TPU v7x, 32 devices: a whole 2x2x4 slice. The times are simulated.
32 devices in a mesh: grp: 8 (over z, x), box: 4 (over y, core).
Axes of the slice: x: 2, y: 2, z: 4, core: 2. Of those that a mesh axis runs over, the one named last changes fastest.
Arguments:
- source_term: float32 [53, 8, 8, 256], P(None, 'grp', 'box'), may hold values from -24 to 24
- diffusion: float32 [53], replicated, may hold values from 0.1 to 2
- stoich: float32 [53, 325], replicated, may hold values from -0.3125 to 0.3125
- orders: float32 [325, 53], replicated, may hold values from -0.875 to 0.875
- rates: float32 [325, 8, 8, 256], P(None, 'grp', 'box'), may hold values from 0.1 to 1
- precond: bfloat16 [53, 53, 8, 8, 256], P(None, None, 'grp', 'box'), may hold values from -1 to 1
- coarse_field: float32 [53, 8, 1024], P(None, 'grp', 'box'), may hold values from -6 to 6
- neighbours: int32 [8, 4], replicated, may hold values from -1 to 7, as said below
- ghost_list: int32 [8, 4, 160], P(None, 'box'), may hold values from -1 to 2047, as said below
- average_list: int32 [8, 4], P(None, 'box'), may hold values from 0 to 31, as said below
Outputs:
- correction: float32 [53, 8, 8, 256], P(None, 'grp', 'box')
- coarse_update: float32 [53, 8, 1024], P(None, 'grp', 'box')
Inputs may be any that keep to these rules, and one draw needn't show every extreme that they name: Column g sits at one position of a grid 4 columns wide and 2 rows tall, each position taken once; neighbours[g, 0] and neighbours[g, 1] are the columns before and after it in its grid row, neighbours[g, 2] and neighbours[g, 3] the ones in the grid rows below and above, -1 at the grid's edge. The relation is symmetric: neighbours[neighbours[g, f], f xor 1] = g. `ghost_list`: an entry is -1 exactly where its face meets another fine sub-box: the lower x face for b > 0, the upper x face for b < 3, side face f where neighbours[g, f] >= 0. Every other entry is o * 256 + c, coarse cell c of the patch of column o at the same box index. `average_list`: entry o * 4 + j names block j of the patch of column o at the same box index; at each box index the 8 entries are distinct.
All inputs are finite; a program needn't handle non-finite values.
Results may differ from a plain program's by a relative error of at most 0.0007.
Values sent between devices are 32-bit elements; how exact they have to be, the bound alone decides.
A program may use at most 64 MiB of HBM per device.

v0:
```python
import jax
import jax.numpy as jnp
from jax import lax
from jax.sharding import PartitionSpec as P

FS = 16
ITERS = 4


EXACT = lax.Precision.HIGHEST


def extended_2(cells, sides, width):
    for axis, dim in sides:
        count = lax.axis_size(axis)
        ends = count - 1
        head = lax.slice_in_dim(cells, 0, width, axis=dim)
        tail = lax.slice_in_dim(cells, cells.shape[dim] - width, cells.shape[dim], axis=dim)
        cells = jnp.concatenate(
            [
                lax.ppermute(tail, axis, [(i, (i + 1) % count) for i in range(ends)]),
                cells,
                lax.ppermute(head, axis, [((i + 1) % count, i) for i in range(ends)]),
            ],
            axis=dim,
        )
    return cells


def face_planes(core, side):
    return (core[..., :side], core[..., -side:], core[..., 0::side], core[..., side - 1 :: side])


def neighbour_sum(core, x_lower, x_upper, sides, side):
    padded = jnp.concatenate([x_lower[..., None, :], core, x_upper[..., None, :]], axis=-2)
    total = padded[..., :-2, :] + padded[..., 2:, :]
    total = total + jnp.concatenate([core[..., side:], sides[1]], axis=-1)
    total = total + jnp.concatenate([sides[0], core[..., :-side]], axis=-1)
    column = jnp.arange(core.shape[-1]) % side
    blank = jnp.zeros(core.shape[:-1] + (1,), core.dtype)
    ahead = jnp.concatenate([core[..., 1:], blank], axis=-1)
    behind = jnp.concatenate([blank, core[..., :-1]], axis=-1)
    total = total + jnp.where(column == side - 1, jnp.repeat(sides[3], side, axis=-1), ahead)
    total = total + jnp.where(column == 0, jnp.repeat(sides[2], side, axis=-1), behind)
    return total


def least_squares(columns, beta):
    count = len(columns)
    target = [beta] + [jnp.zeros_like(beta)] * count
    rotations = []
    upper = []
    for j in range(count):
        entries = list(columns[j])
        for i in range(j):
            cosine_part, sine_part = rotations[i]
            first = cosine_part * entries[i] + sine_part * entries[i + 1]
            second = cosine_part * entries[i + 1] - sine_part * entries[i]
            entries[i] = first
            entries[i + 1] = second
        radius = jnp.sqrt(entries[j] * entries[j] + entries[j + 1] * entries[j + 1])
        cosine_part = entries[j] / radius
        sine_part = entries[j + 1] / radius
        rotations.append((cosine_part, sine_part))
        entries[j] = radius
        target[j + 1] = -sine_part * target[j]
        target[j] = cosine_part * target[j]
        upper.append(entries[: j + 1])
    result = [None] * count
    for j in reversed(range(count)):
        running = target[j]
        for k in range(j + 1, count):
            running = running - upper[k][j] * result[k]
        result[j] = running / upper[j][j]
    return result


def on_device(
    source_term,
    diffusion,
    stoich,
    orders,
    rates,
    precond,
    coarse_field,
    neighbours,
    ghost_list,
    average_list,
):
    species = source_term.shape[0]
    slab = source_term.shape[2]
    face = source_term.shape[3]
    side = FS
    half = side // 2
    group_index = lax.axis_index("grp")
    field_shape = (species, slab, face)
    diffuse = diffusion[:, None, None]
    inverse = precond.reshape(species, species, slab, face)
    reaction = rates.reshape(rates.shape[0], slab * face)
    links = lax.dynamic_index_in_dim(neighbours, group_index, 0, keepdims=False)
    linked = links >= 0
    partner = jnp.maximum(links, 0)

    def global_norm(field):
        return jnp.sqrt(lax.psum(jnp.sum(field * field), ("grp", "box")))

    own_list = lax.dynamic_index_in_dim(ghost_list[:, 0, :], group_index, 0, keepdims=False)
    patch = coarse_field[:, 0, :]
    patch_size = patch.shape[1]
    every_patch = lax.all_gather(coarse_field, "grp", axis=1, tiled=True).reshape(species, -1)
    values = jnp.take(every_patch, jnp.maximum(own_list, 0), axis=1)
    values = jnp.where(own_list[None, :] >= 0, values, 0.0)
    face_ids = jnp.arange(face)
    x_index = face_ids // side // 2 * half + face_ids % side // 2
    side_ids = jnp.arange(slab * side)
    side_index = (side_ids // side // 2 * half + side_ids % side // 2).reshape(slab, side)
    x_slots = half * half
    side_slots = slab // 2 * half
    lower_x = values[:, :x_slots][:, x_index]
    upper_x = values[:, x_slots : 2 * x_slots][:, x_index]
    sides = tuple(
        (
            values[:, 2 * x_slots + f * side_slots : 2 * x_slots + (f + 1) * side_slots][
                :, side_index
            ]
            for f in range(4)
        )
    )
    boundary = diffuse * neighbour_sum(
        jnp.zeros(field_shape, jnp.float32), lower_x, upper_x, sides, side
    )
    right = source_term.reshape(field_shape) + boundary
    beta = global_norm(right)
    basis = [right / beta]
    directions = []
    columns = []
    for j in range(ITERS):
        direction = jnp.einsum(
            "ijxc,jxc->ixc", inverse, basis[j], preferred_element_type=jnp.float32, precision=EXACT
        )
        directions.append(direction)
        extended = extended_2(direction, (("box", 1),), 1)
        planes = jnp.stack(face_planes(direction, side))
        every = lax.all_gather(planes[None], "grp", axis=0, tiled=True)
        picked = every[partner, jnp.array([1, 0, 3, 2])]
        picked = jnp.where(linked[:, None, None, None], picked, 0.0)
        beside_all = neighbour_sum(
            direction,
            extended[:, 0],
            extended[:, -1],
            (picked[0], picked[1], picked[2], picked[3]),
            side,
        )
        progress = jnp.dot(orders, direction.reshape(species, -1), precision=EXACT)
        chemistry = jnp.dot(stoich, reaction * progress, precision=EXACT).reshape(field_shape)
        image = direction + diffuse * (6.0 * direction - beside_all) - chemistry
        local = jnp.stack([jnp.sum(basis[i] * image) for i in range(j + 1)])
        summed = lax.psum(local, ("grp", "box"))
        heights = [summed[i] for i in range(j + 1)]
        for i in range(j + 1):
            image = image - heights[i] * basis[i]
        length = global_norm(image)
        columns.append(heights + [length])
        if j + 1 < ITERS:
            basis.append(image / length)
    weights = least_squares(columns, beta)
    correction = sum((weights[j] * directions[j] for j in range(ITERS)))
    cells = slab * face
    cell_ids = jnp.arange(cells)
    plane = cell_ids // face
    within = cell_ids % face
    block = slab // 2 * half * half
    target = plane // 2 * (half * half) + within // side // 2 * half + within % side // 2
    averaging = (target[:, None] == jnp.arange(block)[None, :]).astype(jnp.float32)
    averaged = jnp.dot(correction.reshape(species, cells), averaging, precision=EXACT) * 0.125
    every_average = lax.all_gather(averaged[:, None, :], "grp", axis=1, tiled=True)
    slot_count = patch_size // block
    wanted = group_index * slot_count + jnp.arange(slot_count)
    select = (average_list[None, :, 0] == wanted[:, None]).astype(jnp.float32)
    blocks = jnp.einsum("jp,spk->sjk", select, every_average, precision=EXACT)
    covered = jnp.sum(select, axis=1) > 0
    updated = jnp.where(covered[None, :, None], blocks, patch.reshape(species, slot_count, block))
    return (correction.reshape(species, 1, slab, face), updated.reshape(species, 1, patch_size))


def solution(mesh):
    placed = (
        P(None, "grp", "box", None),
        P(),
        P(),
        P(),
        P(None, "grp", "box", None),
        P(None, None, "grp", "box", None),
        P(None, "grp", "box"),
        P(),
        P(None, "box", None),
        P(None, "box"),
    )
    return jax.shard_map(
        on_device,
        mesh=mesh,
        in_specs=placed,
        out_specs=(P(None, "grp", "box", None), P(None, "grp", "box")),
        check_vma=False,
    )
```

profile of v0, /device:TPU:0, one launch (start us, length us, event | category | flops | bytes accessed | tf_op | source)
XLA Modules:
  0.0 698.8 jit_solution(17997828659540701746)
XLA Ops:
  2.2 32.8 %all_gather.18 = f32[53,8,256]{2,0,1:T(8,128)S(1)} all-gather(f32[53,1,256]{2,0,1:T(8,128)S(1)} %copy.150), channel_id=1, replica_groups=mesh['grp'=8,'box'=4] {'grp'}, dimensions={1}, use_global_device_ids=true | all-gather | bytes 488448 | tf_op jit(solution)/shard_map/all_gather | solution.py:110
  42.6 39.9 %psum.63 = f32[]{:T(128)} all-reduce(f32[]{:T(128)} %get-tuple-element.30), channel_id=1, replica_groups=mesh['grp'=8,'box'=4] {'grp','box'}, use_global_device_ids=true, to_apply=%region_1.2 | all-reduce | flops 1 | bytes 8 | tf_op jit(solution)/shard_map/psum | solution.py:105
  83.2 11.9 %copy.160 = bf16[53,53,2,256]{0,1,3,2:T(8,128)(2,1)} copy(bf16[53,53,2,256]{3,2,1,0:T(2,128)(2,1)} %bitcast.309) | data formatting | bytes 5752832 | tf_op jit(solution)/shard_map/reshape | solution.py:98
  95.2 8.4 %fusion.96 = f32[2,256,1,53]{3,2,1,0:T(1,128)S(1)} fusion(f32[53,2,256,1]{0,3,2,1:T(1,128)S(1)} %bitcast.331, bf16[53,53,2,256]{0,1,3,2:T(8,128)(2,1)} %copy.160), kind=kOutput, calls=%fused_computation.260 | convolution fusion | flops 17258496 | bytes 3093504 | tf_op jit(solution)/shard_map/ijxc,jxc->ixc/dot_general | solution.py:138
  106.7 31.4 %all-gather = f32[32,53,2,16]{1,3,2,0:T(8,128)S(1)} all-gather(f32[4,53,2,16]{1,3,2,0:T(8,128)S(1)} %pad_maximum_fusion.8), channel_id=2, replica_groups=mesh['grp'=8,'box'=4] {'grp'}, dimensions={0}, use_global_device_ids=true | all-gather | bytes 244224 | tf_op jit(solution)/shard_map/all_gather | solution.py:144
  145.8 41.2 %psum.64 = f32[]{:T(128)} all-reduce(f32[]{:T(128)} %get-tuple-element.28), channel_id=1, replica_groups=mesh['grp'=8,'box'=4] {'grp','box'}, use_global_device_ids=true, to_apply=%region_3.4 | all-reduce | flops 1 | bytes 8 | tf_op jit(solution)/shard_map/psum | solution.py:158
  189.2 42.7 %psum.65 = f32[]{:T(128)} all-reduce(f32[]{:T(128)} %multiply_reduce_fusion.12), channel_id=1, replica_groups=mesh['grp'=8,'box'=4] {'grp','box'}, use_global_device_ids=true, to_apply=%region_5.6 | all-reduce | flops 1 | bytes 8 | tf_op jit(solution)/shard_map/psum | solution.py:105
  233.4 8.4 %fusion.97 = f32[2,256,1,53]{3,2,1,0:T(1,128)S(1)} fusion(f32[53,2,256,1]{0,3,2,1:T(1,128)S(1)} %bitcast.308, bf16[53,53,2,256]{0,1,3,2:T(8,128)(2,1)} %copy.160), kind=kOutput, calls=%fused_computation.261 | convolution fusion | flops 17258496 | bytes 3093504 | tf_op jit(solution)/shard_map/ijxc,jxc->ixc/dot_general | solution.py:138
  242.7 31.4 %all-gather.1 = f32[32,53,2,16]{1,3,2,0:T(8,128)S(1)} all-gather(f32[4,53,2,16]{1,3,2,0:T(8,128)S(1)} %pad_maximum_fusion.9), channel_id=3, replica_groups=mesh['grp'=8,'box'=4] {'grp'}, dimensions={0}, use_global_device_ids=true | all-gather | bytes 244224 | tf_op jit(solution)/shard_map/all_gather | solution.py:144
  281.0 2.8 collective-permute-done.3
  287.1 39.0 %psum.66 = f32[2]{0:T(128)S(1)} all-reduce(f32[2]{0:T(128)S(1)} %pad_maximum_fusion.12), channel_id=1, replica_groups=mesh['grp'=8,'box'=4] {'grp','box'}, use_global_device_ids=true, to_apply=%region_8.9 | all-reduce | flops 2 | bytes 16 | tf_op jit(solution)/shard_map/psum | solution.py:158
  328.8 42.3 %psum.67 = f32[]{:T(128)} all-reduce(f32[]{:T(128)} %get-tuple-element.25), channel_id=1, replica_groups=mesh['grp'=8,'box'=4] {'grp','box'}, use_global_device_ids=true, to_apply=%region_10.11 | all-reduce | flops 1 | bytes 8 | tf_op jit(solution)/shard_map/psum | solution.py:105
  371.8 8.4 %fusion.98 = f32[2,256,1,53]{3,2,1,0:T(1,128)S(1)} fusion(f32[53,2,256,1]{0,3,2,1:T(1,128)S(1)} %bitcast.332, bf16[53,53,2,256]{0,1,3,2:T(8,128)(2,1)} %copy.160), kind=kOutput, calls=%fused_computation.262 | convolution fusion | flops 17258496 | bytes 3093504 | tf_op jit(solution)/shard_map/ijxc,jxc->ixc/dot_general | solution.py:138
  381.9 31.4 %all-gather.2 = f32[32,53,2,16]{1,3,2,0:T(8,128)S(1)} all-gather(f32[4,53,2,16]{1,3,2,0:T(8,128)S(1)} %pad_maximum_fusion.10), channel_id=4, replica_groups=mesh['grp'=8,'box'=4] {'grp'}, dimensions={0}, use_global_device_ids=true | all-gather | bytes 244224 | tf_op jit(solution)/shard_map/all_gather | solution.py:144
  427.0 39.1 %psum.68 = f32[3]{0:T(128)S(1)} all-reduce(f32[3]{0:T(128)S(1)} %pad_maximum_fusion.13), channel_id=1, replica_groups=mesh['grp'=8,'box'=4] {'grp','box'}, use_global_device_ids=true, to_apply=%region_14.15 | all-reduce | flops 3 | bytes 24 | tf_op jit(solution)/shard_map/psum | solution.py:158
  466.8 2.7 multiply_reduce_fusion.5
  469.5 42.3 %psum.69 = f32[]{:T(128)} all-reduce(f32[]{:T(128)} %get-tuple-element.22), channel_id=1, replica_groups=mesh['grp'=8,'box'=4] {'grp','box'}, use_global_device_ids=true, to_apply=%region_16.17 | all-reduce | flops 1 | bytes 8 | tf_op jit(solution)/shard_map/psum | solution.py:105
  512.5 8.4 %fusion.99 = f32[2,256,1,53]{3,2,1,0:T(1,128)S(1)} fusion(f32[53,2,256,1]{0,3,2,1:T(1,128)S(1)} %bitcast.330, bf16[53,53,2,256]{0,1,3,2:T(8,128)(2,1)} %copy.160), kind=kOutput, calls=%fused_computation.263 | convolution fusion | flops 17258496 | bytes 3093504 | tf_op jit(solution)/shard_map/ijxc,jxc->ixc/dot_general | solution.py:138
  522.6 33.4 %all-gather.3 = f32[32,53,2,16]{1,3,2,0:T(8,128)} all-gather(f32[4,53,2,16]{1,3,2,0:T(8,128)S(1)} %pad_maximum_fusion.11), channel_id=5, replica_groups=mesh['grp'=8,'box'=4] {'grp'}, dimensions={0}, use_global_device_ids=true | all-gather | bytes 244224 | tf_op jit(solution)/shard_map/all_gather | solution.py:144
  569.5 2.5 pad_maximum_fusion.14
  572.1 40.5 %psum.70 = f32[4]{0:T(128)S(1)} all-reduce(f32[4]{0:T(128)S(1)} %pad_maximum_fusion.14), channel_id=1, replica_groups=mesh['grp'=8,'box'=4] {'grp','box'}, use_global_device_ids=true, to_apply=%region_21.22 | all-reduce | flops 4 | bytes 32 | tf_op jit(solution)/shard_map/psum | solution.py:158
  618.3 3.3 multiply_reduce_fusion
  621.6 42.2 %psum.71 = f32[]{:T(128)} all-reduce(f32[]{:T(128)} %multiply_reduce_fusion), channel_id=1, replica_groups=mesh['grp'=8,'box'=4] {'grp','box'}, use_global_device_ids=true, to_apply=%region_23.24 | all-reduce | flops 1 | bytes 8 | tf_op jit(solution)/shard_map/psum | solution.py:105
  665.3 30.7 %all-gather.5 = f32[8,64,53]{1,2,0:T(8,128)S(1)} all-gather(f32[1,64,53]{1,2,0:T(8,128)S(1)} %fusion.5), channel_id=6, replica_groups=mesh['grp'=8,'box'=4] {'grp'}, dimensions={0}, use_global_device_ids=true | all-gather | bytes 122112 | tf_op jit(solution)/shard_map/all_gather | solution.py:176
  (158 shorter events, 62.5 us)
Async XLA Ops:
  0.6 141.3 %copy-start = (f32[325,53]{0,1:T(8,128)S(1)}, f32[325,53]{0,1:T(8,128)}, u32[]{:S(2)}) copy-start(f32[325,53]{0,1:T(8,128)} %param.17) | copy-start | bytes 206704
  36.3 58.9 %copy-start.11 = (pred[256]{0:T(512)(128)(4,1)}, pred[256]{0:T(512)(128)(4,1)S(1)}, u32[]{:S(2)}) copy-start(pred[256]{0:T(512)(128)(4,1)S(1)} %get-tuple-element.99) | copy-start | bytes 772
  36.3 107.9 %copy-start.9 = (pred[256]{0:T(512)(128)(4,1)}, pred[256]{0:T(512)(128)(4,1)S(1)}, u32[]{:S(2)}) copy-start(pred[256]{0:T(512)(128)(4,1)S(1)} %get-tuple-element.98) | copy-start | bytes 772
  95.2 42.9 %copy-start.14 = (s32[8,4]{0,1:T(4,128)S(1)}, s32[8,4]{0,1:T(4,128)}, u32[]{:S(2)}) copy-start(s32[8,4]{0,1:T(4,128)} %param.21) | copy-start | bytes 388
  95.2 43.1 %copy-start.15 = (s32[1,4]{0,1:T(4,128)S(1)}, s32[1,4]{0,1:T(4,128)}, u32[]{:S(2)}) copy-start(s32[1,4]{0,1:T(4,128)} %constant.320) | copy-start | bytes 52
  95.2 45.9 %copy-start.16 = (s32[8,1]{0,1:T(1,128)S(1)}, s32[8,1]{0,1:T(1,128)}, u32[]{:S(2)}) copy-start(s32[8,1]{0,1:T(1,128)} %param.23) | copy-start | bytes 100
  103.7 39.0 %copy-start.1 = (f32[53,325]{1,0:T(8,128)S(1)}, f32[53,325]{1,0:T(8,128)}, u32[]{:S(2)}) copy-start(f32[53,325]{1,0:T(8,128)} %param.16) | copy-start | bytes 206704
  103.7 40.3 %copy-start.3 = (f32[53,1,256]{2,1,0:T(1,128)S(1)}, f32[53,1,256]{2,1,0:T(1,128)}, u32[]{:S(2)}) copy-start(f32[53,1,256]{2,1,0:T(1,128)} %param.20) | copy-start | bytes 162820
  103.7 40.5 %copy-start.7 = (f32[53]{0:T(128)S(1)}, f32[53]{0:T(128)}, u32[]{:S(2)}) copy-start(f32[53]{0:T(128)} %param.15) | copy-start | bytes 640
  103.7 40.4 %collective-permute-start = (f32[53,1,256]{0,2,1:T(8,128)S(1)}, f32[53,1,256]{0,2,1:T(8,128)S(1)}, u32[]{:S(2)}, u32[]{:S(2)}) collective-permute-start(f32[53,1,256]{0,2,1:T(8,128)S(1)} %get-tuple-element.58), channel_id=1, source_target_pairs={{0,1},{1,2},{2,3},{4,5},{5,6},{6,7},{8,9},{9,10},{10,11},{12,13},{... | collective-permute-start | bytes 162824 | tf_op jit(solution)/shard_map/ppermute | solution.py:21
  105.2 39.0 %collective-permute-start.1 = (f32[53,1,256]{0,2,1:T(8,128)S(1)}, f32[53,1,256]{0,2,1:T(8,128)S(1)}, u32[]{:S(2)}, u32[]{:S(2)}) collective-permute-start(f32[53,1,256]{0,2,1:T(8,128)S(1)} %get-tuple-element.59), channel_id=1, source_target_pairs={{1,0},{2,1},{3,2},{5,4},{6,5},{7,6},{9,8},{10,9},{11,10},{13,12},{... | collective-permute-start | bytes 162824 | tf_op jit(solution)/shard_map/ppermute | solution.py:23
  141.1 3.1 copy-start.17
  276.2 4.8 collective-permute-start.2
  277.5 6.3 collective-permute-start.3
  281.0 2.8 copy-start.6
  371.8 51.1 %copy-start.8 = (f32[53]{0:T(128)S(1)}, f32[53]{0:T(128)}, u32[]{:S(2)}) copy-start(f32[53]{0:T(128)} %param.15) | copy-start | bytes 640
  371.8 51.1 %copy-start.10 = (pred[256]{0:T(512)(128)(4,1)S(1)}, pred[256]{0:T(512)(128)(4,1)}, u32[]{:S(2)}) copy-start(pred[256]{0:T(512)(128)(4,1)} %copy-done.9) | copy-start | bytes 772
  371.8 51.1 %copy-start.12 = (pred[256]{0:T(512)(128)(4,1)S(1)}, pred[256]{0:T(512)(128)(4,1)}, u32[]{:S(2)}) copy-start(pred[256]{0:T(512)(128)(4,1)} %copy-done.11) | copy-start | bytes 772
  415.3 6.3 collective-permute-start.4
  417.2 5.7 collective-permute-start.5
  520.9 144.0 %copy-start.13 = (s32[512]{0:T(512)S(1)}, s32[512]{0:T(512)}, u32[]{:S(2)}) copy-start(s32[512]{0:T(512)} %fusion.58) | copy-start | bytes 6148
  559.0 6.8 collective-permute-start.6
  560.3 6.3 collective-permute-start.7
  565.7 130.6 %copy-start.2 = (f32[53,4,64]{2,1,0:T(4,128)S(1)}, f32[53,4,64]{2,1,0:T(4,128)}, u32[]{:S(2)}) copy-start(f32[53,4,64]{2,1,0:T(4,128)} %reshape_squeeze.3) | copy-start | bytes 162820
  (2 other events, 1.5 us)
where the time goes:
time: 701 us; the launch traced here: 699 us
  blocking collectives  560 us (80%)
  matrix products  40.5 us (6%)
  local copies, waits for them, and re-layouts  33.9 us (5%)
  other arithmetic  28.8 us (4%)
  between operations  18.9 us (3%)
  starting transfers between devices  11.3 us (2%)
    psum x5, blocking collectives, global_norm(): return jnp.sqrt(lax.psum(jnp.sum(field * field), ('grp', 'box')))  209 us
    psum x4, blocking collectives, on_device(): summed = lax.psum(local, ('grp', 'box'))  160 us
    all_gather x4, blocking collectives, on_device(): every = lax.all_gather(planes[None], 'grp', axis=0, tiled=True)  128 us
    dot_general x4, matrix products, on_device(): jnp.einsum('ijxc,jxc->ixc', inverse, basis[j], preferred_element_type=jnp...  33.6 us
    all_gather x1, blocking collectives, on_device(): lax.all_gather(coarse_field, 'grp', axis=1, tiled=True).reshape(species, -1)  32.8 us
    all_gather x1, blocking collectives, on_device(): lax.all_gather(averaged[:, None, :], 'grp', axis=1, tiled=True)  30.7 us
  transfers between devices with their start and end apart: 8, of which 3 were waited for; matrix products, arithmetic and copies ran while one was open for 1% of the time, Pallas kernels for 0%

commit v1 on v0

v1 whole, which is shorter than its diff:
```python
import functools

import jax
import jax.numpy as jnp
from jax import lax
from jax.experimental import pallas as pl
from jax.experimental.pallas import tpu as pltpu
from jax.sharding import PartitionSpec as P

ITERS = 4
SP = 64
ROWS = 56
RP = 384
LANES = 128
MESH = pl.DeviceIdType.MESH
F32 = jnp.float32
BF16 = jnp.bfloat16


def least_squares(columns, beta):
    count = len(columns)
    target = [beta] + [jnp.zeros_like(beta)] * count
    rotations = []
    upper = []
    for j in range(count):
        entries = list(columns[j])
        for i in range(j):
            cosine_part, sine_part = rotations[i]
            first = cosine_part * entries[i] + sine_part * entries[i + 1]
            second = cosine_part * entries[i + 1] - sine_part * entries[i]
            entries[i] = first
            entries[i + 1] = second
        radius = jnp.sqrt(entries[j] * entries[j] + entries[j + 1] * entries[j + 1])
        cosine_part = entries[j] / radius
        sine_part = entries[j + 1] / radius
        rotations.append((cosine_part, sine_part))
        entries[j] = radius
        target[j + 1] = -sine_part * target[j]
        target[j] = cosine_part * target[j]
        upper.append(entries[: j + 1])
    result = [None] * count
    for j in reversed(range(count)):
        running = target[j]
        for k in range(j + 1, count):
            running = running - upper[k][j] * result[k]
        result[j] = running / upper[j][j]
    return result


def split(x, parts):
    pieces = []
    for _ in range(parts - 1):
        piece = x.astype(BF16)
        pieces.append(piece)
        x = x - piece.astype(F32)
    pieces.append(x.astype(BF16))
    return pieces


def dot(a, b):
    return jnp.dot(a, b, preferred_element_type=F32)


def exact_dot(x, ones, parts):
    rows = x.shape[0]
    product = dot(jnp.concatenate(split(x, parts), axis=0), ones)
    return sum(product[i * rows : (i + 1) * rows] for i in range(parts))


def iota(shape, dim):
    return lax.broadcasted_iota(jnp.int32, shape, dim)


def cell_of(index):
    k, l = index >> 7, index & 127
    return k >> 1, ((k & 1) << 3) + (l >> 4), l & 15


def on_face(face, t, y, z):
    return (
        ((face == 0) & (y == 0) & (z == t))
        | ((face == 1) & (y == 15) & (z == t))
        | ((face == 2) & (z == 0) & (y == t))
        | ((face == 3) & (z == 15) & (y == t))
    )


def ones_where(condition):
    return jnp.where(condition, 1.0, 0.0).astype(BF16)


def padded(x):
    return jnp.concatenate([x, jnp.zeros((SP - x.shape[0], x.shape[1]), F32)], axis=0)


def fields(x):
    return [x[:, k * LANES : (k + 1) * LANES] for k in range(4)]


def kernel(
    groups, boxes, species, reactions,
    neighbours, average_list, ghosts, source, diffusion, stoich, orders, rates, coarse, precond,
    correction_out, coarse_out,
    raw, wide, even, odd, applied, direct, basis, rate, stage, order_cat, stoich_cat, pick, spread,
    ghost_send, ghost_recv, plane_send, plane_recv, x_recv, red_send, red_recv, mean_send, mean_recv,
    load_sem, ghost_ssem, ghost_rsem, plane_ssem, plane_rsem, x_ssem, x_rsem,
    red_ssem, red_rsem, mean_ssem, mean_rsem,
):
    g = lax.axis_index("grp")
    b = lax.axis_index("box")
    load = pltpu.make_async_copy(precond, raw, load_sem)
    load.start()
    barrier = pltpu.get_barrier_semaphore()

    def grp_peer(k):
        return (lax.rem(g + k, groups), b)

    def box_peer(k):
        return (g, lax.rem(b + k, boxes))

    for k in range(1, groups):
        pl.semaphore_signal(barrier, inc=1, device_id=grp_peer(k), device_id_type=MESH)
    for k in range(1, boxes):
        pl.semaphore_signal(barrier, inc=1, device_id=box_peer(k), device_id_type=MESH)

    def remote(src, dst, ssem, rsem, device):
        return pltpu.make_async_remote_copy(
            src_ref=src, dst_ref=dst, send_sem=ssem, recv_sem=rsem,
            device_id=device, device_id_type=MESH,
        )

    stage[...] = jnp.zeros_like(stage)
    stage[0:species, 0:256] = coarse[...]
    patch = jnp.concatenate(split(stage[:, 0:256], 3), axis=0)
    cell = iota((256, LANES), 0) + g * 256

    def chosen(k):
        wanted = ghosts[pl.ds(lax.rem(g + k, groups), 1), :]
        got = dot(patch, ones_where(cell == wanted))
        return got[0:SP] + got[SP : 2 * SP] + got[2 * SP :]

    for k in range(1, groups):
        ghost_send[k - 1] = chosen(k)[0:ROWS]
    own_ghosts = chosen(0)
    pl.semaphore_wait(barrier, groups + boxes - 2)
    ghost_copies = [
        remote(ghost_send.at[k - 1], ghost_recv.at[k - 1], ghost_ssem.at[k - 1],
               ghost_rsem.at[k - 1], grp_peer(k))
        for k in range(1, groups)
    ]
    for copy in ghost_copies:
        copy.start()

    even[...] = jnp.zeros_like(even)
    odd[...] = jnp.zeros_like(odd)
    applied[...] = jnp.zeros_like(applied)
    rate[...] = jnp.zeros_like(rate)
    for x in range(2):
        for ct in range(2):
            k = 2 * x + ct
            rate[0:reactions, k * LANES : (k + 1) * LANES] = rates[
                pl.ds(2 * ct + x, reactions, stride=4), :
            ]
    order_cat[...] = jnp.zeros_like(order_cat)
    order_cat[0:reactions, 0:species] = orders[...]
    whole = order_cat[...]
    high = whole.astype(BF16).astype(F32)
    low = whole - high
    order_parts = jnp.concatenate([high + pltpu.roll(low, 64, 1), high], axis=1).astype(BF16)
    stage[...] = jnp.zeros_like(stage)
    stage[0:species, 0:reactions] = stoich[...]
    whole = stage[:, 0:RP]
    stoich_high, stoich_low = split(whole, 2)
    stoich_cat[0:SP, :] = stoich_high
    stoich_cat[SP : 2 * SP, :] = stoich_low
    x, y, z = cell_of(iota((512, LANES), 0))
    slot = iota((512, LANES), 1)
    pick[...] = ones_where(((slot >> 4 & 1) == x) & on_face(slot >> 5, slot & 15, y, z))
    x, y, z = cell_of(iota((LANES, 512), 1))
    slot = iota((LANES, 512), 0)
    spread[...] = ones_where(((slot >> 4 & 1) == x) & on_face(slot >> 5, slot & 15, y, z))
    end = jnp.where(b == 0, 0, 1)
    behind_x = (slot < 64) & (x == end) & (((y >> 1) << 3) + (z >> 1) == slot)
    past = slot - 64
    face = past >> 3
    t = jnp.where(face < 2, z, y)
    behind_side = (slot >= 64) & (slot < 96) & ((t >> 1) == (past & 7)) & on_face(face, t, y, z)
    coarse_spread = ones_where(behind_x | behind_side)

    load.wait()
    count = species * species * 4
    chunk = 432
    steps = count // chunk

    def widen(i, carry):
        at = pl.multiple_of(i * chunk, 16)
        wide[pl.ds(at, chunk), :] = raw[pl.ds(at, chunk), :].astype(F32)
        return carry

    lax.fori_loop(0, steps, widen, 0)
    tail = steps * chunk
    wide[tail:, :] = jnp.zeros((wide.shape[0] - tail, LANES), F32)
    wide[tail:count, :] = raw[tail:count, :].astype(F32)

    diffuse = jnp.concatenate([padded(diffusion[...])] * 4, axis=1)
    stage[...] = jnp.zeros_like(stage)
    for x in range(2):
        for ct in range(2):
            k = 2 * x + ct
            stage[0:species, k * LANES : (k + 1) * LANES] = source[
                pl.ds(2 * ct + x, species, stride=4), :
            ]
    for copy in ghost_copies:
        copy.wait_recv()
    values = own_ghosts[0:ROWS]
    for k in range(1, groups):
        values = values + ghost_recv[k - 1]
    basis[0] = stage[...] + diffuse * exact_dot(padded(values), coarse_spread, 3)

    half = species // 2

    def apply_inverse(v):
        for x in range(2):
            for ct in range(2):
                part = v[0:ROWS, (2 * x + ct) * LANES : (2 * x + ct + 1) * LANES]
                even[pl.ds(2 * ct + x, ROWS, stride=4), :] = part
                odd[pl.ds(4 + 2 * ct + x, ROWS, stride=4), :] = part
        rows = 4 * species + 4
        low_half = iota((8, LANES), 0) < 4

        def product(at, vector):
            p = (wide[pl.ds(pl.multiple_of(at, 8), rows), :] * vector[0:rows, :]).reshape(
                rows // 8, 8, LANES
            )
            parts = [p[i] for i in range(rows // 8)]
            while len(parts) > 1:
                pairs = [a + c for a, c in zip(parts[0::2], parts[1::2])]
                parts = pairs + ([parts[-1]] if len(parts) % 2 else [])
            return parts[0] + pltpu.roll(parts[0], 4, 0)

        def pair(m, carry):
            at = m * (8 * species)
            applied[pl.ds(pl.multiple_of(m * 8, 8), 8), :] = jnp.where(
                low_half, product(at, even), product(at + 4 * species - 4, odd)
            )
            return carry

        lax.fori_loop(0, half, pair, 0)
        applied[8 * half : 8 * half + 8, :] = jnp.where(
            low_half, product(half * 8 * species, even), 0.0
        )
        return [
            padded(applied[pl.ds(2 * ct + x, ROWS, stride=4), :])
            for x in range(2)
            for ct in range(2)
        ]

    lane = iota((16, LANES), 1)
    wide_lane = iota((SP, LANES), 1)
    links = [neighbours[g, f] for f in range(4)]

    def rolled(x, shift):
        shift = shift % LANES
        return pltpu.roll(x, shift, 1) if shift else x

    def side_messages(flat):
        planes = exact_dot(flat, pick[...], 2)
        packed = []
        for f in range(4):
            total = jnp.zeros((16, LANES), F32)
            for q in range(4):
                rows = planes[16 * q : 16 * q + 16]
                total = jnp.where((lane >> 5) == q, rolled(rows, 32 * (q - f)), total)
            packed.append(total)
        for k in range(1, groups):
            peer = lax.rem(g + k, groups)
            message = jnp.zeros((16, LANES), F32)
            for f in range(4):
                message = jnp.where(links[f] == peer, packed[f], message)
            plane_send[k - 1] = message

    def side_ghosts():
        found = [jnp.zeros((16, LANES), F32)] * 4
        for k in range(1, groups):
            peer = lax.rem(g + groups - k, groups)
            message = plane_recv[k - 1]
            found = [
                jnp.where(links[f] == peer, message, found[f]) for f in range(4)
            ]
        rows = []
        for q in range(4):
            total = jnp.zeros((16, LANES), F32)
            for f in range(4):
                total = jnp.where((lane >> 5) == f, rolled(found[f], 32 * (f - q)), total)
            rows.append(total)
        return exact_dot(jnp.concatenate(rows, axis=0), spread[...], 2)

    def inner_sum(d):
        result = []
        zero = jnp.zeros((SP, LANES), F32)
        z = wide_lane & 15
        for x in range(2):
            plane = d[2 * x : 2 * x + 2]
            up = [rolled(p, -16) for p in plane]
            down = [rolled(p, 16) for p in plane]
            for ct in range(2):
                own = plane[ct]
                total = d[2 * (1 - x) + ct]
                total = total + jnp.where(z == 15, 0.0, rolled(own, -1))
                total = total + jnp.where(z == 0, 0.0, rolled(own, 1))
                total = total + jnp.where(wide_lane >= 112, up[1] if ct == 0 else zero, up[ct])
                total = total + jnp.where(wide_lane < 16, down[0] if ct == 1 else zero, down[ct])
                result.append(total)
        return result

    def row_of(a, c):
        p = a * c
        p = p[:, 0:128] + p[:, 128:256] + p[:, 256:384] + p[:, 384:512]
        return jnp.sum(p, axis=0, keepdims=True)

    def all_reduce(rows, turn):
        at = turn % 2
        row_id = iota((8, LANES), 0)
        tile = jnp.zeros((8, LANES), F32)
        for i, row in enumerate(rows):
            tile = jnp.where(row_id == i, row, tile)
        first = 0
        for stage_id, (size, peer) in enumerate(((boxes, box_peer), (groups, grp_peer))):
            red_send[at, stage_id] = tile
            copies = [
                remote(red_send.at[at, stage_id], red_recv.at[at, first + k - 1],
                       red_ssem.at[at, first + k - 1], red_rsem.at[at, first + k - 1], peer(k))
                for k in range(1, size)
            ]
            for copy in copies:
                copy.start()
            for copy in copies:
                copy.wait_recv()
            for k in range(1, size):
                tile = tile + red_recv[at, first + k - 1]
            for copy in copies:
                copy.wait_send()
            first += size - 1
        sums = jnp.sum(tile, axis=1, keepdims=True)
        return [sums[i : i + 1] for i in range(len(rows))]

    for copy in ghost_copies:
        copy.wait_send()

    squares = []
    lengths = []
    columns = []
    for j in range(ITERS):
        d = apply_inverse(basis[j])
        for k in range(4):
            direct[j, k] = d[k]
        up = remote(direct.at[j, 2:4, 0:ROWS], x_recv.at[0], x_ssem.at[0], x_rsem.at[0],
                    (g, lax.rem(b + 1, boxes)))
        down = remote(direct.at[j, 0:2, 0:ROWS], x_recv.at[1], x_ssem.at[1], x_rsem.at[1],
                      (g, lax.rem(b + boxes - 1, boxes)))
        pl.when(b < boxes - 1)(up.start)
        pl.when(b > 0)(down.start)
        flat = jnp.concatenate(d, axis=1)
        side_messages(flat)
        plane_copies = [
            remote(plane_send.at[k - 1], plane_recv.at[k - 1], plane_ssem.at[k - 1],
                   plane_rsem.at[k - 1], grp_peer(k))
            for k in range(1, groups)
        ]
        for copy in plane_copies:
            copy.start()

        d_high, d_low = split(flat, 2)
        d_cat = jnp.concatenate([d_high, d_high, d_low, jnp.zeros_like(d_low)], axis=0)
        progress = rate[...] * dot(order_parts, d_cat)
        q_high, q_low = split(progress, 2)
        both = dot(stoich_cat[...], q_high)
        chemistry = both[0:SP] + both[SP:] + dot(stoich_cat[0:SP, :], q_low)
        inner = jnp.concatenate(inner_sum(d), axis=1)
        image = flat + diffuse * (6.0 * flat - inner) - chemistry

        pl.when(b > 0)(up.wait_recv)
        pl.when(b < boxes - 1)(down.wait_recv)
        zero = jnp.zeros((ROWS, LANES), F32)
        outer = [padded(jnp.where(b > 0, x_recv[0, ct], zero)) for ct in range(2)]
        outer += [padded(jnp.where(b < boxes - 1, x_recv[1, ct], zero)) for ct in range(2)]
        for copy in plane_copies:
            copy.wait_recv()
        image = image - diffuse * (jnp.concatenate(outer, axis=1) + side_ghosts())

        known = [basis[i] for i in range(j + 1)]
        rows = [row_of(known[j], known[j])] + [row_of(v, image) for v in known]
        sums = all_reduce(rows, j)
        pl.when(b < boxes - 1)(up.wait_send)
        pl.when(b > 0)(down.wait_send)
        for copy in plane_copies:
            copy.wait_send()
        squares.append(sums[0])
        lengths.append(jnp.sqrt(sums[0]))
        columns.append([sums[1 + i] / (lengths[i] * lengths[j]) for i in range(j + 1)])
        for i in range(j + 1):
            image = image - (sums[1 + i] / squares[i]) * known[i]
        basis[j + 1] = image / lengths[j]

    last = basis[ITERS]
    lengths.append(jnp.sqrt(all_reduce([row_of(last, last)], ITERS)[0]))
    for j in range(ITERS):
        columns[j].append(lengths[j + 1])
    weights = least_squares(columns, lengths[0])
    scales = [weights[j] / lengths[j] for j in range(ITERS)]
    total = [sum(scales[j] * direct[j, k] for j in range(ITERS)) for k in range(4)]
    cell = iota((256, LANES), 0)
    slot = iota((256, LANES), 1) & 63
    to_slot = (((((cell >> 7) << 3) + ((cell & 127) >> 4)) >> 1) << 3) + ((cell & 15) >> 1)
    pair_sum = jnp.concatenate([total[0] + total[2], total[1] + total[3]], axis=1)
    mean = exact_dot(pair_sum, ones_where(to_slot == slot), 3)[0:ROWS] * 0.125
    mean_send[...] = mean
    mean_copies = [
        remote(mean_send, mean_recv.at[k - 1], mean_ssem.at[k - 1], mean_rsem.at[k - 1], grp_peer(k))
        for k in range(1, groups)
    ]
    for copy in mean_copies:
        copy.start()
    for x in range(2):
        for ct in range(2):
            correction_out[pl.ds(2 * ct + x, species, stride=4), :] = total[2 * x + ct][0:species]
    for copy in mean_copies:
        copy.wait_recv()
    left = iota((ROWS, LANES), 1) < 64
    stage[...] = jnp.zeros_like(stage)
    stage[0:species, 0:256] = coarse[...]
    for c in range(2):
        block = stage[0:ROWS, c * LANES : (c + 1) * LANES]
        for k in range(groups):
            entry = average_list[lax.rem(g + groups - k, groups), 0] - (4 * g + 2 * c)
            message = mean if k == 0 else mean_recv[k - 1]
            block = jnp.where((left & (entry == 0)) | (~left & (entry == 1)), message, block)
        coarse_out[:, c * LANES : (c + 1) * LANES] = block[0:species]
    for copy in mean_copies:
        copy.wait_send()


def on_device(
    groups, boxes,
    source_term, diffusion, stoich, orders, rates, precond, coarse_field,
    neighbours, ghost_list, average_list,
):
    species = source_term.shape[0]
    reactions = rates.shape[0]

    def rows_of(x):
        lead = x.shape[:-3]
        x = x.reshape(lead + (2, 2, LANES))
        n = len(lead)
        x = x.transpose(tuple(range(n)) + (n + 1, n, n + 2))
        return x.reshape(-1, LANES)

    b = lax.axis_index("box")
    lists = ghost_list[:, 0, :]
    ghosts = jnp.concatenate(
        [
            jnp.where(b == 0, lists[:, 0:64], lists[:, 64:128]),
            lists[:, 128:160],
            jnp.full((groups, 32), -1, jnp.int32),
        ],
        axis=1,
    )
    vmem = pl.BlockSpec(memory_space=pltpu.VMEM)
    smem = pl.BlockSpec(memory_space=pltpu.SMEM)
    count = 4 * species * species
    dma = pltpu.SemaphoreType.DMA
    reds = groups + boxes - 2
    correction, updated = pl.pallas_call(
        functools.partial(kernel, groups, boxes, species, reactions),
        out_shape=(
            jax.ShapeDtypeStruct((4 * species, LANES), F32),
            jax.ShapeDtypeStruct((species, 256), F32),
        ),
        in_specs=[smem, smem] + [vmem] * 7 + [pl.BlockSpec(memory_space=pl.ANY)],
        out_specs=(vmem, vmem),
        scratch_shapes=[
            pltpu.VMEM((count, LANES), BF16),
            pltpu.VMEM((count + 4, LANES), F32),
            pltpu.VMEM((224, LANES), F32),
            pltpu.VMEM((232, LANES), F32),
            pltpu.VMEM((224, LANES), F32),
            pltpu.VMEM((ITERS, 4, SP, LANES), F32),
            pltpu.VMEM((ITERS + 1, SP, 512), F32),
            pltpu.VMEM((RP, 512), F32),
            pltpu.VMEM((SP, 512), F32),
            pltpu.VMEM((RP, LANES), F32),
            pltpu.VMEM((2 * SP, RP), BF16),
            pltpu.VMEM((512, LANES), BF16),
            pltpu.VMEM((LANES, 512), BF16),
            pltpu.VMEM((groups - 1, ROWS, LANES), F32),
            pltpu.VMEM((groups - 1, ROWS, LANES), F32),
            pltpu.VMEM((groups - 1, 16, LANES), F32),
            pltpu.VMEM((groups - 1, 16, LANES), F32),
            pltpu.VMEM((2, 2, ROWS, LANES), F32),
            pltpu.VMEM((2, 2, 8, LANES), F32),
            pltpu.VMEM((2, reds, 8, LANES), F32),
            pltpu.VMEM((ROWS, LANES), F32),
            pltpu.VMEM((groups - 1, ROWS, LANES), F32),
            dma,
            dma((groups - 1,)),
            dma((groups - 1,)),
            dma((groups - 1,)),
            dma((groups - 1,)),
            dma((2,)),
            dma((2,)),
            dma((2, reds)),
            dma((2, reds)),
            dma((groups - 1,)),
            dma((groups - 1,)),
        ],
        compiler_params=pltpu.CompilerParams(
            collective_id=0, has_side_effects=True, vmem_limit_bytes=40 * 1024 * 1024
        ),
        name="gmres",
    )(
        neighbours,
        average_list,
        ghosts,
        rows_of(source_term),
        jnp.broadcast_to(diffusion[:, None], (species, LANES)),
        stoich,
        orders,
        rows_of(rates),
        coarse_field.reshape(species, 256),
        rows_of(precond),
    )
    correction = correction.reshape(species, 2, 2, LANES).transpose(0, 2, 1, 3)
    return (
        correction.reshape(species, 1, 2, 256),
        updated.reshape(species, 1, 256),
    )


def solution(mesh):
    placed = (
        P(None, "grp", "box", None),
        P(),
        P(),
        P(),
        P(None, "grp", "box", None),
        P(None, None, "grp", "box", None),
        P(None, "grp", "box"),
        P(),
        P(None, "box", None),
        P(None, "box"),
    )
    return jax.shard_map(
        functools.partial(on_device, mesh.shape["grp"], mesh.shape["box"]),
        mesh=mesh,
        in_specs=placed,
        out_specs=(P(None, "grp", "box", None), P(None, "grp", "box")),
        check_vma=False,
    )
```

time: 701 us -> 104 us (0.15)
  blocking collectives: 560 us -> 0 us
  Pallas kernels: 0 us -> 77.1 us
  matrix products: 40.5 us -> 0 us
  other arithmetic: 28.8 us -> 0.15 us
  between operations: 18.9 us -> 0.69 us
  starting transfers between devices: 11.3 us -> 0 us
  local copies, waits for them, and re-layouts: 33.9 us -> 25.7 us
    psum x9 -> x0, blocking collectives: 369 us -> none  [the longest x5 209 us: global_norm(): return jnp.sqrt(lax.psum(jnp.sum(field * field), ('grp', 'box')))]
    all_gather x6 -> x0, blocking collectives: 191 us -> none  [the longest x4 128 us: on_device(): every = lax.all_gather(planes[None], 'grp', axis=0, tiled=True)]
    pallas_call x0 -> x1, Pallas kernels: none -> 77.1 us  [on_device(): pl.pallas_call(functools.partial(kernel, groups, boxes, species, reaction...]
    dot_general x14 -> x0, matrix products: 40.5 us -> none  [the longest x4 33.6 us: on_device(): jnp.einsum('ijxc,jxc->ixc', inverse, basis[j], preferred_element_type=jnp...]
    reduce_sum x10 -> x0, other arithmetic: 19.2 us -> none  [the longest x5 10.9 us: global_norm(): return jnp.sqrt(lax.psum(jnp.sum(field * field), ('grp', 'box')))]
    ppermute x8 -> x0, starting transfers between devices: 11.3 us -> none  [the longest x4 5.97 us: extended_2(): lax.ppermute(tail, axis, [(i, (i + 1) % count) for i in range(ends)])]
    unnamed x42 -> x22, local copies, waits for them, and re-layouts: 4.83 us -> 13.6 us
    gather x11 -> x0, local copies, waits for them, and re-layouts: 7.71 us -> none  [the longest x4 3.27 us: on_device(): picked = every[partner, jnp.array([1, 0, 3, 2])]]
  transfers between devices with their start and end apart: 8 -> 0, of which waited for: 3 -> 0; matrix products, arithmetic and copies ran while one was open for 1% -> 0% of each run, Pallas kernels for 0% -> 0%
where the time goes in v1:
time: 104 us
  Pallas kernels  77.1 us (74%)
  local copies, waits for them, and re-layouts  25.7 us (25%)
    pallas_call x1, Pallas kernels, on_device(): pl.pallas_call(functools.partial(kernel, groups, boxes, species, reaction...  77.1 us
    unnamed x22, local copies, waits for them, and re-layouts  13.6 us
    reshape x3, local copies, waits for them, and re-layouts, rows_of(): return x.reshape(-1, LANES)  9.1 us

profile of v1, /device:TPU:0, one launch (start us, length us, event | category | flops | bytes accessed | tf_op | source)
XLA Modules:
  0.0 103.6 jit_solution(14596220461086399447)
XLA Ops:
  0.6 0.1 pad.2.clone
  0.7 0.8 copy.15.neighbours
  1.5 1.3 %copy.16.average_list = s32[8,1]{1,0:T(8,128)} copy(s32[8,1]{0,1:T(1,128)} %param.19) | data formatting | bytes 64 | tf_op args[9]
  2.8 0.7 copy.25
  3.5 0.1 slice_select_fusion
  3.6 0.1 add_add_fusion.ghosts
  3.7 1.3 %broadcast_in_dim.10.diffusion = f32[53,128]{1,0:T(8,128)} broadcast(f32[53]{0:T(128)} %param.11), dimensions={0} | broadcast | bytes 27348 | tf_op jit(solution)/shard_map/broadcast_in_dim | solution.py:525
  5.0 1.4 %copy.24 = f32[53,1,256]{2,0,1:T(8,128)} copy(f32[53,1,256]{2,1,0:T(1,128)} %param.16) | data formatting | bytes 108544
  6.4 1.6 %reshape.36.source = f32[212,128]{1,0:T(8,128)} reshape(f32[53,2,2,128]{3,2,1,0:T(2,128)} %bitcast.23) | data formatting | bytes 217088 | tf_op jit(solution)/shard_map/reshape | solution.py:456
  8.1 1.7 %copy.17.orders = f32[325,53]{1,0:T(8,128)} copy(f32[325,53]{0,1:T(8,128)} %param.13) | data formatting | bytes 137800 | tf_op args[3]
  9.7 1.5 %reshape.38.rates = f32[1300,128]{1,0:T(8,128)S(1)} reshape(f32[325,2,2,128]{3,2,1,0:T(2,128)} %bitcast.22) | data formatting | bytes 1331200 | tf_op jit(solution)/shard_map/reshape | solution.py:456
  11.3 5.9 %reshape.41.precond = bf16[11236,128]{1,0:T(8,128)(2,1)S(1)} reshape(bf16[53,53,2,2,128]{4,3,2,1,0:T(2,128)(2,1)} %bitcast.21) | data formatting | bytes 5752832 | tf_op jit(solution)/shard_map/reshape | solution.py:456
  17.2 0.0 copy-start
  17.2 0.9 copy-done
  18.1 0.9 copy-done.1
  19.0 0.8 copy-done.2
  19.8 0.7 copy-done.3
  20.6 0.9 copy-done.5
  21.5 0.7 copy-done.7
  22.2 77.1 %gmres.1 = (f32[212,128]{1,0:T(8,128)S(1)}, f32[53,256]{1,0:T(8,128)S(1)}) custom-call(s32[8,4]{1,0:T(8,128)S(1)} %copy.15.neighbours, s32[8,1]{1,0:T(8,128)S(1)} %copy-done.7, s32[8,128]{1,0:T(8,128)S(1)} %add_add_fusion.ghosts, f32[212,128]{1,0:T(8,128)S(1)} %copy-done.1, f32[53,128]{1,0:T(8,128)S(1)} %copy-done.3, f32[53,325]{1,0:T(8,128)S(1)} %copy-done.5, ...), custom_call_target="tpu_custom_call" | custom-call | tf_op jit(solution)/shard_map/gmres/pallas_call | solution.py:473
  99.2 0.6 copy-done.4
  99.9 0.6 copy-done.6
  100.5 1.6 %reshape.42 = f32[53,2,2,128]{3,2,1,0:T(2,128)} reshape(f32[212,128]{1,0:T(8,128)} %copy-done.4) | data formatting | bytes 217088 | tf_op jit(solution)/shard_map/reshape | solution.py:532
  102.1 1.5 %copy.19 = f32[53,1,256]{2,1,0:T(1,128)} copy(f32[53,1,256]{2,0,1:T(8,128)} %bitcast.20) | data formatting | bytes 108544
  (9 shorter events, 0.0 us)
Async XLA Ops:
  17.2 0.9 copy-start
  18.1 0.9 copy-start.1
  19.0 0.8 copy-start.2
  19.8 0.7 copy-start.3
  20.6 0.9 copy-start.5
  21.5 0.7 copy-start.7
  99.2 0.7 copy-start.4
  99.9 0.6 copy-start.6

commit v2 on v1

v2 whole, which is shorter than its diff:
```python
import functools

import jax
import jax.numpy as jnp
from jax import lax
from jax.experimental import pallas as pl
from jax.experimental.pallas import tpu as pltpu
from jax.sharding import PartitionSpec as P

ITERS = 4
SP = 64
ROWS = 56
RP = 384
LANES = 128
MESH = pl.DeviceIdType.MESH
F32 = jnp.float32
BF16 = jnp.bfloat16


def rotated(columns, beta):
    count = len(columns)
    target = [beta] + [jnp.zeros_like(beta)] * (count - 1)
    rotations = []
    upper = []
    for j in range(count):
        entries = list(columns[j])
        for i in range(j):
            cosine_part, sine_part = rotations[i]
            first = cosine_part * entries[i] + sine_part * entries[i + 1]
            second = cosine_part * entries[i + 1] - sine_part * entries[i]
            entries[i] = first
            entries[i + 1] = second
        upper.append(entries)
        if j + 1 == count:
            return upper, target, entries[j]
        radius = jnp.sqrt(entries[j] * entries[j] + entries[j + 1] * entries[j + 1])
        cosine_part = entries[j] / radius
        sine_part = entries[j + 1] / radius
        rotations.append((cosine_part, sine_part))
        entries[j] = radius
        target[j + 1] = -sine_part * target[j]
        target[j] = cosine_part * target[j]


def back_substitute(upper, target, final):
    count = len(upper)
    result = [None] * (count - 1) + [final]
    for j in reversed(range(count - 1)):
        running = target[j]
        for k in range(j + 1, count):
            running = running - upper[k][j] * result[k]
        result[j] = running / upper[j][j]
    return result


def split(x, parts):
    pieces = []
    for _ in range(parts - 1):
        piece = x.astype(BF16)
        pieces.append(piece)
        x = x - piece.astype(F32)
    pieces.append(x.astype(BF16))
    return pieces


def dot(a, b):
    return jnp.dot(a, b, preferred_element_type=F32)


def exact_dot(x, ones, parts):
    rows = x.shape[0]
    product = dot(jnp.concatenate(split(x, parts), axis=0), ones)
    return sum(product[i * rows : (i + 1) * rows] for i in range(parts))


def iota(shape, dim):
    return lax.broadcasted_iota(jnp.int32, shape, dim)


def cell_of(index):
    k, l = index >> 7, index & 127
    return k >> 1, ((k & 1) << 3) + (l >> 4), l & 15


def on_face(face, t, y, z):
    return (
        ((face == 0) & (y == 0) & (z == t))
        | ((face == 1) & (y == 15) & (z == t))
        | ((face == 2) & (z == 0) & (y == t))
        | ((face == 3) & (z == 15) & (y == t))
    )


def ones_where(condition):
    return jnp.where(condition, 1.0, 0.0).astype(BF16)


def padded(x):
    return jnp.concatenate([x, jnp.zeros((SP - x.shape[0], x.shape[1]), F32)], axis=0)


def fields(x):
    return [x[:, k * LANES : (k + 1) * LANES] for k in range(4)]


def kernel(
    groups, boxes, species, reactions,
    neighbours, average_list, ghost_list, source, diffusion, stoich, orders, rates, coarse, precond,
    correction_out, coarse_out,
    raw, wide, even, odd, applied, direct, images, basis, rate, stage, tall, stoich_cat, pick, spread,
    lists, wanted_cells, source_raw, diffusion_raw, stoich_raw, orders_raw, rates_raw, coarse_raw, flow, patch_new,
    x_send, ghost_send, ghost_recv, plane_send, plane_recv, x_recv, red_send, red_recv,
    mean_send, mean_recv,
    load_sem, ghost_ssem, ghost_rsem, plane_ssem, plane_rsem, x_ssem, x_rsem,
    red_ssem, red_rsem, mean_ssem, mean_rsem,
):
    g = lax.axis_index("grp")
    b = lax.axis_index("box")
    barrier = pltpu.get_barrier_semaphore()

    def grp_peer(k):
        return (lax.rem(g + k, groups), b)

    def box_peer(k):
        return (g, lax.rem(b + k, boxes))

    for k in range(1, groups):
        pl.semaphore_signal(barrier, inc=1, device_id=grp_peer(k), device_id_type=MESH)
    for k in range(1, boxes):
        pl.semaphore_signal(barrier, inc=1, device_id=box_peer(k), device_id_type=MESH)

    def remote(src, dst, ssem, rsem, device):
        return pltpu.make_async_remote_copy(
            src_ref=src, dst_ref=dst, send_sem=ssem, recv_sem=rsem,
            device_id=device, device_id_type=MESH,
        )

    loads = [
        pltpu.make_async_copy(src, dst, load_sem.at[i])
        for i, (src, dst) in enumerate((
            (ghost_list.at[:, 0, :], lists),
            (coarse.at[:, 0, :], coarse_raw),
            (precond.reshape(4 * species * species, LANES), raw),
            (rates.reshape(4 * reactions, LANES), rates_raw),
            (orders, orders_raw),
            (stoich, stoich_raw),
            (diffusion, diffusion_raw),
            (source.reshape(4 * species, LANES), source_raw),
        ))
    ]
    for load in loads:
        load.start()

    stage[...] = jnp.zeros_like(stage)
    loads[0].wait()
    loads[1].wait()
    stage[0:species, 0:256] = coarse_raw[...]
    x_slots = lists[:, 0:LANES]
    x_slots = jnp.where(b == 0, x_slots, pltpu.roll(x_slots, 64, 1))
    side_slots = jnp.concatenate(
        [
            jnp.full((groups, 64), -1, jnp.int32),
            lists[:, LANES : LANES + 32],
            jnp.full((groups, 32), -1, jnp.int32),
        ],
        axis=1,
    )
    wanted_cells[...] = jnp.where(iota((groups, LANES), 1) < 64, x_slots, side_slots)
    patch = jnp.concatenate(split(stage[:, 0:256], 3), axis=0)
    cell = iota((256, LANES), 0) + g * 256

    def chosen(k):
        wanted = wanted_cells[pl.ds(lax.rem(g + k, groups), 1), :]
        got = dot(patch, ones_where(cell == wanted))
        return got[0:SP] + got[SP : 2 * SP] + got[2 * SP :]

    for k in range(1, groups):
        ghost_send[k - 1] = chosen(k)[0:ROWS]
    own_ghosts = chosen(0)
    pl.semaphore_wait(barrier, groups + boxes - 2)
    ghost_copies = [
        remote(ghost_send.at[k - 1], ghost_recv.at[k - 1], ghost_ssem.at[k - 1],
               ghost_rsem.at[k - 1], grp_peer(k))
        for k in range(1, groups)
    ]
    for copy in ghost_copies:
        copy.start()

    even[...] = jnp.zeros_like(even)
    odd[...] = jnp.zeros_like(odd)
    applied[...] = jnp.zeros_like(applied)
    rate[...] = jnp.zeros_like(rate)
    for load in loads[3:]:
        load.wait()
    for x in range(2):
        for ct in range(2):
            k = 2 * x + ct
            rate[0:reactions, k * LANES : (k + 1) * LANES] = rates_raw[
                pl.ds(2 * ct + x, reactions, stride=4), :
            ]
    tall[...] = jnp.zeros_like(tall)
    tall[0:species, 0:reactions] = orders_raw[...]
    whole = tall[...].T
    high = whole.astype(BF16).astype(F32)
    low = whole - high
    order_parts = jnp.concatenate([high + pltpu.roll(low, 64, 1), high], axis=1).astype(BF16)
    stage[...] = jnp.zeros_like(stage)
    stage[0:species, 0:reactions] = stoich_raw[...]
    whole = stage[:, 0:RP]
    stoich_high, stoich_low = split(whole, 2)
    stoich_cat[0:SP, :] = stoich_high
    stoich_cat[SP : 2 * SP, :] = stoich_low
    x, y, z = cell_of(iota((512, LANES), 0))
    slot = iota((512, LANES), 1)
    pick[...] = ones_where(((slot >> 4 & 1) == x) & on_face(slot >> 5, slot & 15, y, z))
    x, y, z = cell_of(iota((LANES, 512), 1))
    slot = iota((LANES, 512), 0)
    spread[...] = ones_where(((slot >> 4 & 1) == x) & on_face(slot >> 5, slot & 15, y, z))
    end = jnp.where(b == 0, 0, 1)
    behind_x = (slot < 64) & (x == end) & (((y >> 1) << 3) + (z >> 1) == slot)
    past = slot - 64
    face = past >> 3
    t = jnp.where(face < 2, z, y)
    behind_side = (slot >= 64) & (slot < 96) & ((t >> 1) == (past & 7)) & on_face(face, t, y, z)
    coarse_spread = ones_where(behind_x | behind_side)

    loads[2].wait()
    count = species * species * 4
    chunk = 432
    steps = count // chunk

    def widen(i, carry):
        at = pl.multiple_of(i * chunk, 16)
        wide[pl.ds(at, chunk), :] = raw[pl.ds(at, chunk), :].astype(F32)
        return carry

    lax.fori_loop(0, steps, widen, 0)
    tail = steps * chunk
    wide[tail:, :] = jnp.zeros((wide.shape[0] - tail, LANES), F32)
    wide[tail:count, :] = raw[tail:count, :].astype(F32)

    tall[0:8, 0:LANES] = jnp.zeros((8, LANES), F32)
    tall[0:1, 0:species] = diffusion_raw[...]
    same = iota((SP, LANES), 0) == iota((SP, LANES), 1)
    diffuse = jnp.sum(jnp.where(same, tall[0:1, 0:LANES], 0.0), axis=1, keepdims=True)
    diffuse = jnp.broadcast_to(diffuse, (SP, 512))
    stage[...] = jnp.zeros_like(stage)
    for x in range(2):
        for ct in range(2):
            k = 2 * x + ct
            stage[0:species, k * LANES : (k + 1) * LANES] = source_raw[
                pl.ds(2 * ct + x, species, stride=4), :
            ]
    for copy in ghost_copies:
        copy.wait_recv()
    values = own_ghosts[0:ROWS]
    for k in range(1, groups):
        values = values + ghost_recv[k - 1]
    basis[0] = stage[...] + diffuse * exact_dot(padded(values), coarse_spread, 3)

    half = species // 2

    def apply_inverse(v):
        for x in range(2):
            for ct in range(2):
                part = v[0:ROWS, (2 * x + ct) * LANES : (2 * x + ct + 1) * LANES]
                even[pl.ds(2 * ct + x, ROWS, stride=4), :] = part
                odd[pl.ds(4 + 2 * ct + x, ROWS, stride=4), :] = part
        rows = 4 * species + 4
        low_half = iota((8, LANES), 0) < 4

        def product(at, vector):
            p = (wide[pl.ds(pl.multiple_of(at, 8), rows), :] * vector[0:rows, :]).reshape(
                rows // 8, 8, LANES
            )
            parts = [p[i] for i in range(rows // 8)]
            while len(parts) > 1:
                pairs = [a + c for a, c in zip(parts[0::2], parts[1::2])]
                parts = pairs + ([parts[-1]] if len(parts) % 2 else [])
            return parts[0] + pltpu.roll(parts[0], 4, 0)

        def pair(m, carry):
            at = m * (8 * species)
            applied[pl.ds(pl.multiple_of(m * 8, 8), 8), :] = jnp.where(
                low_half, product(at, even), product(at + 4 * species - 4, odd)
            )
            return carry

        def two_pairs(m, carry):
            return pair(2 * m + 1, pair(2 * m, carry))

        lax.fori_loop(0, half // 2, two_pairs, 0)
        if half % 2:
            pair(half - 1, 0)
        applied[8 * half : 8 * half + 8, :] = jnp.where(
            low_half, product(half * 8 * species, even), 0.0
        )
        return [
            padded(applied[pl.ds(2 * ct + x, ROWS, stride=4), :])
            for x in range(2)
            for ct in range(2)
        ]

    lane = iota((16, LANES), 1)
    wide_lane = iota((SP, LANES), 1)
    links = [neighbours[f, g] for f in range(4)]

    def rolled(x, shift):
        shift = shift % LANES
        return pltpu.roll(x, shift, 1) if shift else x

    def side_messages(flat, at):
        planes = exact_dot(flat, pick[...], 2)
        packed = []
        for f in range(4):
            total = jnp.zeros((16, LANES), F32)
            for q in range(4):
                rows = planes[16 * q : 16 * q + 16]
                total = jnp.where((lane >> 5) == q, rolled(rows, 32 * (q - f)), total)
            packed.append(total)
        for k in range(1, groups):
            peer = lax.rem(g + k, groups)
            message = jnp.zeros((16, LANES), F32)
            for f in range(4):
                message = jnp.where(links[f] == peer, packed[f], message)
            plane_send[at, k - 1] = message

    def side_ghosts(at):
        found = [jnp.zeros((16, LANES), F32)] * 4
        for k in range(1, groups):
            peer = lax.rem(g + groups - k, groups)
            message = plane_recv[at, k - 1]
            found = [
                jnp.where(links[f] == peer, message, found[f]) for f in range(4)
            ]
        rows = []
        for q in range(4):
            total = jnp.zeros((16, LANES), F32)
            for f in range(4):
                total = jnp.where((lane >> 5) == f, rolled(found[f], 32 * (f - q)), total)
            rows.append(total)
        return exact_dot(jnp.concatenate(rows, axis=0), spread[...], 2)

    def inner_sum(d):
        result = []
        zero = jnp.zeros((SP, LANES), F32)
        z = wide_lane & 15
        for x in range(2):
            plane = d[2 * x : 2 * x + 2]
            up = [rolled(p, -16) for p in plane]
            down = [rolled(p, 16) for p in plane]
            for ct in range(2):
                own = plane[ct]
                total = d[2 * (1 - x) + ct]
                total = total + jnp.where(z == 15, 0.0, rolled(own, -1))
                total = total + jnp.where(z == 0, 0.0, rolled(own, 1))
                total = total + jnp.where(wide_lane >= 112, up[1] if ct == 0 else zero, up[ct])
                total = total + jnp.where(wide_lane < 16, down[0] if ct == 1 else zero, down[ct])
                result.append(total)
        return result

    def row_of(a, c):
        p = a * c
        p = p[:, 0:128] + p[:, 128:256] + p[:, 256:384] + p[:, 384:512]
        return jnp.sum(p, axis=0, keepdims=True)

    def reduce_stage(tile, turn, stage_id):
        at = turn % 2
        first, size, peer = ((0, boxes, box_peer), (boxes - 1, groups, grp_peer))[stage_id]
        red_send[at, stage_id] = tile
        copies = [
            remote(red_send.at[at, stage_id], red_recv.at[at, first + k - 1],
                   red_ssem.at[at, first + k - 1], red_rsem.at[at, first + k - 1], peer(k))
            for k in range(1, size)
        ]
        for copy in copies:
            copy.start()

        def finish():
            total = tile
            for copy in copies:
                copy.wait_recv()
            for k in range(1, size):
                total = total + red_recv[at, first + k - 1]
            for copy in copies:
                copy.wait_send()
            return total

        return finish

    def reduce_rows(rows, turn):
        row_id = iota((8, LANES), 0)
        tile = jnp.zeros((8, LANES), F32)
        for i, row in enumerate(rows):
            tile = jnp.where(row_id == i, row, tile)
        return reduce_stage(tile, turn, 0)

    def sums_of(tile):
        return jnp.sum(tile, axis=1, keepdims=True)

    def send_halo(v, turn):
        at = turn % 2
        d = apply_inverse(v)
        for k in range(4):
            x_send[at, k] = d[k]
        up = remote(x_send.at[at, 2:4, 0:ROWS], x_recv.at[at, 0], x_ssem.at[at, 0],
                    x_rsem.at[at, 0], (g, lax.rem(b + 1, boxes)))
        down = remote(x_send.at[at, 0:2, 0:ROWS], x_recv.at[at, 1], x_ssem.at[at, 1],
                      x_rsem.at[at, 1], (g, lax.rem(b + boxes - 1, boxes)))
        pl.when(b < boxes - 1)(up.start)
        pl.when(b > 0)(down.start)
        flat = jnp.concatenate(d, axis=1)
        side_messages(flat, at)
        plane_copies = [
            remote(plane_send.at[at, k - 1], plane_recv.at[at, k - 1], plane_ssem.at[at, k - 1],
                   plane_rsem.at[at, k - 1], grp_peer(k))
            for k in range(1, groups)
        ]
        for copy in plane_copies:
            copy.start()

        def finish():
            d_high, d_low = split(flat, 2)
            d_cat = jnp.concatenate([d_high, d_high, d_low, jnp.zeros_like(d_low)], axis=0)
            progress = rate[...] * dot(order_parts, d_cat)
            q_high, q_low = split(progress, 2)
            both = dot(stoich_cat[...], q_high)
            chemistry = both[0:SP] + both[SP:] + dot(stoich_cat[0:SP, :], q_low)
            inner = jnp.concatenate(inner_sum(d), axis=1)
            image = flat + diffuse * (6.0 * flat - inner) - chemistry
            pl.when(b > 0)(up.wait_recv)
            pl.when(b < boxes - 1)(down.wait_recv)
            zero = jnp.zeros((ROWS, LANES), F32)
            outer = [padded(jnp.where(b > 0, x_recv[at, 0, ct], zero)) for ct in range(2)]
            outer += [
                padded(jnp.where(b < boxes - 1, x_recv[at, 1, ct], zero)) for ct in range(2)
            ]
            for copy in plane_copies:
                copy.wait_recv()
            image = image - diffuse * (jnp.concatenate(outer, axis=1) + side_ghosts(at))
            pl.when(b < boxes - 1)(up.wait_send)
            pl.when(b > 0)(down.wait_send)
            for copy in plane_copies:
                copy.wait_send()
            return image

        return flat, finish

    for copy in ghost_copies:
        copy.wait_send()

    direct[0], finish = send_halo(basis[0], 0)
    images[0] = finish()
    squares = []
    lengths = []
    columns = []
    for j in range(ITERS):
        more = j + 1 < ITERS
        image = images[j]
        known = [basis[i] for i in range(j + 1)]
        rows = [row_of(known[j], known[j])] + [row_of(v, image) for v in known]
        box_sums = reduce_rows(rows, j)
        if more:
            ahead, finish = send_halo(image, j + 1)
        all_sums = reduce_stage(box_sums(), j, 1)
        if more:
            ahead_image = finish()
        sums = sums_of(all_sums())
        sums = [sums[i : i + 1] for i in range(j + 2)]
        squares.append(sums[0])
        lengths.append(jnp.sqrt(sums[0]))
        columns.append([sums[1 + i] / (lengths[i] * lengths[j]) for i in range(j + 1)])
        parts = [sums[1 + i] / (squares[i] * lengths[j]) for i in range(j + 1)]
        scale = 1.0 / lengths[j]

        def corrected(field, past):
            field = field * scale
            for i in range(j + 1):
                field = field - parts[i] * past[i]
            return field

        basis[j + 1] = corrected(image, known)
        if more:
            direct[j + 1] = corrected(ahead, [direct[i] for i in range(j + 1)])
            images[j + 1] = corrected(ahead_image, [images[i] for i in range(j + 1)])

    last = basis[ITERS]
    box_sums = reduce_rows([row_of(last, last)], ITERS)
    for j in range(ITERS - 1):
        columns[j].append(lengths[j + 1])
    upper, target, ending = rotated(columns, lengths[0])
    none = jnp.zeros_like(lengths[0])
    fixed = back_substitute(upper, target, none)
    slope = back_substitute(upper, [none] * ITERS, none + 1.0)
    means = []
    cell = iota((256, LANES), 0)
    slot = iota((256, LANES), 1) & 63
    to_slot = (((((cell >> 7) << 3) + ((cell & 127) >> 4)) >> 1) << 3) + ((cell & 15) >> 1)
    for solved in (fixed, slope):
        total = sum((solved[j] / lengths[j]) * direct[j] for j in range(ITERS))
        means.append(total[:, 0:256] + total[:, 256:512])
    mean = exact_dot(jnp.concatenate(means, axis=0), ones_where(to_slot == slot), 3) * 0.125
    left = iota((ROWS, LANES), 1) < 64
    mean_send[...] = jnp.where(left, mean[0:ROWS], mean[SP : SP + ROWS])
    all_sums = reduce_stage(box_sums(), ITERS, 1)
    mean_copies = [
        remote(mean_send, mean_recv.at[k - 1], mean_ssem.at[k - 1], mean_rsem.at[k - 1], grp_peer(k))
        for k in range(1, groups)
    ]
    for copy in mean_copies:
        copy.start()
    length = jnp.sqrt(sums_of(all_sums())[0:1])
    radius = jnp.sqrt(ending * ending + length * length)
    final = (ending / radius) * target[ITERS - 1] / radius
    weights = back_substitute(upper, target, final)
    total = sum((weights[j] / lengths[j]) * direct[j] for j in range(ITERS))
    for x in range(2):
        for ct in range(2):
            k = 2 * x + ct
            flow[pl.ds(2 * ct + x, species, stride=4), :] = total[
                0:species, k * LANES : (k + 1) * LANES
            ]
    flow_copy = pltpu.make_async_copy(
        flow, correction_out.reshape(4 * species, LANES), load_sem.at[0]
    )
    flow_copy.start()
    for copy in mean_copies:
        copy.wait_recv()
    stage[...] = jnp.zeros_like(stage)
    stage[0:species, 0:256] = coarse_raw[...]
    blocks = [stage[0:ROWS, c * LANES : (c + 1) * LANES] for c in range(2)]
    for k in range(groups):
        message = mean_send[...] if k == 0 else mean_recv[k - 1]
        turned = pltpu.roll(message, 64, 1)
        message = jnp.where(left, message + final * turned, turned + final * message)
        for c in range(2):
            entry = average_list[0, lax.rem(g + groups - k, groups)] - (4 * g + 2 * c)
            blocks[c] = jnp.where(
                (left & (entry == 0)) | (~left & (entry == 1)), message, blocks[c]
            )
    for c in range(2):
        patch_new[:, c * LANES : (c + 1) * LANES] = blocks[c][0:species]
    patch_copy = pltpu.make_async_copy(patch_new, coarse_out.at[:, 0, :], load_sem.at[1])
    patch_copy.start()
    for copy in mean_copies:
        copy.wait_send()
    flow_copy.wait()
    patch_copy.wait()


def on_device(
    groups, boxes,
    source_term, diffusion, stoich, orders, rates, precond, coarse_field,
    neighbours, ghost_list, average_list,
):
    species = source_term.shape[0]
    reactions = rates.shape[0]

    def rows_of(x):
        lead = x.shape[:-3]
        x = x.reshape(lead + (2, 2, LANES))
        n = len(lead)
        x = x.transpose(tuple(range(n)) + (n + 1, n, n + 2))
        return x.reshape(-1, 2, LANES)

    hbm = pl.BlockSpec(memory_space=pl.ANY)
    smem = pl.BlockSpec(memory_space=pltpu.SMEM)
    count = 4 * species * species
    dma = pltpu.SemaphoreType.DMA
    reds = groups + boxes - 2
    correction, updated = pl.pallas_call(
        functools.partial(kernel, groups, boxes, species, reactions),
        out_shape=(
            jax.ShapeDtypeStruct((2 * species, 2, LANES), F32),
            jax.ShapeDtypeStruct((species, 1, 256), F32),
        ),
        in_specs=[smem, smem] + [hbm] * 8,
        out_specs=(hbm, hbm),
        scratch_shapes=[
            pltpu.VMEM((count, LANES), BF16),
            pltpu.VMEM((count + 4, LANES), F32),
            pltpu.VMEM((224, LANES), F32),
            pltpu.VMEM((232, LANES), F32),
            pltpu.VMEM((224, LANES), F32),
            pltpu.VMEM((ITERS, SP, 512), F32),
            pltpu.VMEM((ITERS, SP, 512), F32),
            pltpu.VMEM((ITERS + 1, SP, 512), F32),
            pltpu.VMEM((RP, 512), F32),
            pltpu.VMEM((SP, 512), F32),
            pltpu.VMEM((LANES, RP), F32),
            pltpu.VMEM((2 * SP, RP), BF16),
            pltpu.VMEM((512, LANES), BF16),
            pltpu.VMEM((LANES, 512), BF16),
            pltpu.VMEM((groups, 160), jnp.int32),
            pltpu.VMEM((groups, LANES), jnp.int32),
            pltpu.VMEM((4 * species, LANES), F32),
            pltpu.VMEM((1, species), F32),
            pltpu.VMEM((species, reactions), F32),
            pltpu.VMEM((species, reactions), F32),
            pltpu.VMEM((4 * reactions, LANES), F32),
            pltpu.VMEM((species, 256), F32),
            pltpu.VMEM((4 * species, LANES), F32),
            pltpu.VMEM((species, 256), F32),
            pltpu.VMEM((2, 4, SP, LANES), F32),
            pltpu.VMEM((groups - 1, ROWS, LANES), F32),
            pltpu.VMEM((groups - 1, ROWS, LANES), F32),
            pltpu.VMEM((2, groups - 1, 16, LANES), F32),
            pltpu.VMEM((2, groups - 1, 16, LANES), F32),
            pltpu.VMEM((2, 2, 2, ROWS, LANES), F32),
            pltpu.VMEM((2, 2, 8, LANES), F32),
            pltpu.VMEM((2, reds, 8, LANES), F32),
            pltpu.VMEM((ROWS, LANES), F32),
            pltpu.VMEM((groups - 1, ROWS, LANES), F32),
            dma((8,)),
            dma((groups - 1,)),
            dma((groups - 1,)),
            dma((2, groups - 1)),
            dma((2, groups - 1)),
            dma((2, 2)),
            dma((2, 2)),
            dma((2, reds)),
            dma((2, reds)),
            dma((groups - 1,)),
            dma((groups - 1,)),
        ],
        compiler_params=pltpu.CompilerParams(
            collective_id=0, has_side_effects=True, vmem_limit_bytes=63 * 1024 * 1024
        ),
        name="gmres",
    )(
        neighbours.T,
        average_list.T,
        ghost_list,
        rows_of(source_term),
        diffusion.reshape(1, species),
        stoich,
        orders.T,
        rows_of(rates),
        coarse_field,
        rows_of(precond),
    )
    correction = correction.reshape(species, 2, 2, LANES).transpose(0, 2, 1, 3)
    return (correction.reshape(species, 1, 2, 256), updated)


def solution(mesh):
    placed = (
        P(None, "grp", "box", None),
        P(),
        P(),
        P(),
        P(None, "grp", "box", None),
        P(None, None, "grp", "box", None),
        P(None, "grp", "box"),
        P(),
        P(None, "box", None),
        P(None, "box"),
    )
    return jax.shard_map(
        functools.partial(on_device, mesh.shape["grp"], mesh.shape["box"]),
        mesh=mesh,
        in_specs=placed,
        out_specs=(P(None, "grp", "box", None), P(None, "grp", "box")),
        check_vma=False,
    )
```

time: 104 us -> 61.4 us (0.59)
  local copies, waits for them, and re-layouts: 25.7 us -> 2.98 us
  Pallas kernels: 77.1 us -> 57.6 us
    pallas_call x1, Pallas kernels: 77.1 us -> 57.6 us  [on_device(): pl.pallas_call(functools.partial(kernel, groups, boxes, species, reaction...]
    reshape x4 -> x0, local copies, waits for them, and re-layouts: 10.7 us -> none  [the longest x3 9.1 us: rows_of(): return x.reshape(-1, LANES)]
    unnamed x22 -> x2, local copies, waits for them, and re-layouts: 13.6 us -> 2.98 us
    broadcast_in_dim x2 -> x0, local copies, waits for them, and re-layouts: 1.34 us -> none  [the longest x1 1.34 us: on_device(): jnp.broadcast_to(diffusion[:, None], (species, LANES))]
where the time goes in v2:
time: 61.4 us; the launch traced here: 61.2 us
  Pallas kernels  57.6 us (94%)
  local copies, waits for them, and re-layouts  2.98 us (5%)
  between operations  0.64 us (1%)
    pallas_call x1, Pallas kernels, on_device(): pl.pallas_call(functools.partial(kernel, groups, boxes, species, reaction...  57.6 us
    unnamed x2, local copies, waits for them, and re-layouts  2.98 us

profile of v2, /device:TPU:0, one launch (start us, length us, event | category | flops | bytes accessed | tf_op | source)
XLA Modules:
  0.0 61.2 jit_solution(6990900985417708775)
XLA Ops:
  0.6 57.6 %gmres.1 = (f32[106,2,128]{2,1,0:T(2,128)}, f32[53,1,256]{2,1,0:T(1,128)}) custom-call(s32[4,8]{1,0:T(4,128)} %bitcast.29, s32[1,8]{1,0:T(1,128)} %bitcast.30, s32[8,1,160]{2,1,0:T(1,128)} %ghost_list.1, f32[106,2,128]{2,1,0:T(2,128)} %bitcast.26, f32[1,53]{1,0:T(1,128)} %bitcast.31, f32[53,325]{1,0:T(8,128)} %stoich.1, f32[53,325]{1,0:T(8,128)} %bitcast.28, ...), custom_call_target="tpu_custom_call" | custom-call | tf_op jit(solution)/shard_map/gmres/pallas_call | solution.py:571
  58.2 1.5 %copy.18 = f32[53,1,2,256]{3,2,1,0:T(2,128)} copy(f32[53,1,2,256]{3,2,1,0:T(2,128)} %bitcast.27) | data formatting | bytes 217088
  59.8 1.4 %copy.19 = f32[53,1,256]{2,1,0:T(1,128)} copy(f32[53,1,256]{2,1,0:T(1,128)} %get-tuple-element.9) | data formatting | bytes 108544

commit v3 on v2

--- a/solution.py
+++ b/solution.py
@@ -17,9 +17,9 @@
 BF16 = jnp.bfloat16
 
 
-def rotated(columns, beta):
+def least_squares(columns, beta):
     count = len(columns)
-    target = [beta] + [jnp.zeros_like(beta)] * (count - 1)
+    target = [beta] + [jnp.zeros_like(beta)] * count
     rotations = []
     upper = []
     for j in range(count):
@@ -30,9 +30,6 @@
             second = cosine_part * entries[i + 1] - sine_part * entries[i]
             entries[i] = first
             entries[i + 1] = second
-        upper.append(entries)
-        if j + 1 == count:
-            return upper, target, entries[j]
         radius = jnp.sqrt(entries[j] * entries[j] + entries[j + 1] * entries[j + 1])
         cosine_part = entries[j] / radius
         sine_part = entries[j + 1] / radius
@@ -40,12 +37,9 @@
         entries[j] = radius
         target[j + 1] = -sine_part * target[j]
         target[j] = cosine_part * target[j]
-
-
-def back_substitute(upper, target, final):
-    count = len(upper)
-    result = [None] * (count - 1) + [final]
-    for j in reversed(range(count - 1)):
+        upper.append(entries[: j + 1])
+    result = [None] * count
+    for j in reversed(range(count)):
         running = target[j]
         for k in range(j + 1, count):
             running = running - upper[k][j] * result[k]
@@ -108,7 +102,7 @@
     neighbours, average_list, ghost_list, source, diffusion, stoich, orders, rates, coarse, precond,
     correction_out, coarse_out,
     raw, wide, even, odd, applied, direct, images, basis, rate, stage, tall, stoich_cat, pick, spread,
-    lists, wanted_cells, source_raw, diffusion_raw, stoich_raw, orders_raw, rates_raw, coarse_raw, flow, patch_new,
+    lists, wanted_cells, source_raw, diffusion_raw, stoich_raw, orders_raw, rates_raw, coarse_raw,
     x_send, ghost_send, ghost_recv, plane_send, plane_recv, x_recv, red_send, red_recv,
     mean_send, mean_recv,
     load_sem, ghost_ssem, ghost_rsem, plane_ssem, plane_rsem, x_ssem, x_rsem,
@@ -169,22 +163,47 @@
     patch = jnp.concatenate(split(stage[:, 0:256], 3), axis=0)
     cell = iota((256, LANES), 0) + g * 256
 
+    at_end = (b == 0) | (b == boxes - 1)
+    short = iota((16, LANES), 1)
+    left = iota((32, LANES), 1) < 64
+
     def chosen(k):
         wanted = wanted_cells[pl.ds(lax.rem(g + k, groups), 1), :]
         got = dot(patch, ones_where(cell == wanted))
-        return got[0:SP] + got[SP : 2 * SP] + got[2 * SP :]
+        got = got[0:SP] + got[SP : 2 * SP] + got[2 * SP :]
+        side_part = got[0:16]
+        side_part = pltpu.roll(side_part, 64, 1)
+        for q in range(1, 4):
+            rows = got[16 * q : 16 * q + 16]
+            rows = rows if q == 2 else pltpu.roll(rows, (32 * q - 64) % LANES, 1)
+            side_part = jnp.where((short >> 5) == q, rows, side_part)
+        x_part = jnp.where(left, got[0:32], pltpu.roll(got[32:64], 64, 1))
+        return jnp.concatenate([side_part, x_part], axis=0)
 
     for k in range(1, groups):
-        ghost_send[k - 1] = chosen(k)[0:ROWS]
+        ghost_send[k - 1] = chosen(k)
     own_ghosts = chosen(0)
     pl.semaphore_wait(barrier, groups + boxes - 2)
-    ghost_copies = [
-        remote(ghost_send.at[k - 1], ghost_recv.at[k - 1], ghost_ssem.at[k - 1],
-               ghost_rsem.at[k - 1], grp_peer(k))
-        for k in range(1, groups)
-    ]
-    for copy in ghost_copies:
-        copy.start()
+
+    def ghost_copies(rows):
+        return [
+            remote(ghost_send.at[k - 1, 0:rows], ghost_recv.at[k - 1, 0:rows],
+                   ghost_ssem.at[k - 1], ghost_rsem.at[k - 1], grp_peer(k))
+            for k in range(1, groups)
+        ]
+
+    def for_ghosts(act):
+        @pl.when(at_end)
+        def _():
+            for copy in ghost_copies(48):
+                act(copy)
+
+        @pl.when(jnp.logical_not(at_end))
+        def _():
+            for copy in ghost_copies(16):
+                act(copy)
+
+    for_ghosts(lambda copy: copy.start())
 
     even[...] = jnp.zeros_like(even)
     odd[...] = jnp.zeros_like(odd)
@@ -251,12 +270,25 @@
             stage[0:species, k * LANES : (k + 1) * LANES] = source_raw[
                 pl.ds(2 * ct + x, species, stride=4), :
             ]
-    for copy in ghost_copies:
-        copy.wait_recv()
-    values = own_ghosts[0:ROWS]
+    for_ghosts(lambda copy: copy.wait_recv())
+    side_part = own_ghosts[0:16]
+    x_part = jnp.where(at_end, own_ghosts[16:48], 0.0)
     for k in range(1, groups):
-        values = values + ghost_recv[k - 1]
-    basis[0] = stage[...] + diffuse * exact_dot(padded(values), coarse_spread, 3)
+        side_part = side_part + ghost_recv[k - 1, 0:16]
+        x_part = x_part + jnp.where(at_end, ghost_recv[k - 1, 16:48], 0.0)
+    side_part = jnp.concatenate(
+        [
+            pltpu.roll(side_part, 64, 1),
+            pltpu.roll(side_part, 32, 1),
+            side_part,
+            pltpu.roll(side_part, 96, 1),
+        ],
+        axis=0,
+    )
+    x_part = jnp.concatenate([x_part, pltpu.roll(x_part, 64, 1)], axis=0)
+    place = iota((SP, LANES), 1)
+    values = jnp.where(place < 64, x_part, jnp.where(place < 96, side_part, 0.0))
+    basis[0] = stage[...] + diffuse * exact_dot(values, coarse_spread, 3)
 
     half = species // 2
 
@@ -270,7 +302,7 @@
         low_half = iota((8, LANES), 0) < 4
 
         def product(at, vector):
-            p = (wide[pl.ds(pl.multiple_of(at, 8), rows), :] * vector[0:rows, :]).reshape(
+            p = (wide[pl.ds(pl.multiple_of(at, 8), rows), :] * vector).reshape(
                 rows // 8, 8, LANES
             )
             parts = [p[i] for i in range(rows // 8)]
@@ -279,22 +311,31 @@
                 parts = pairs + ([parts[-1]] if len(parts) % 2 else [])
             return parts[0] + pltpu.roll(parts[0], 4, 0)
 
-        def pair(m, carry):
-            at = m * (8 * species)
-            applied[pl.ds(pl.multiple_of(m * 8, 8), 8), :] = jnp.where(
-                low_half, product(at, even), product(at + 4 * species - 4, odd)
-            )
-            return carry
-
-        def two_pairs(m, carry):
-            return pair(2 * m + 1, pair(2 * m, carry))
-
-        lax.fori_loop(0, half // 2, two_pairs, 0)
-        if half % 2:
-            pair(half - 1, 0)
-        applied[8 * half : 8 * half + 8, :] = jnp.where(
-            low_half, product(half * 8 * species, even), 0.0
-        )
+        def sweep(count, start, vector, store):
+            def step(m, carry):
+                store(m, product(m * (8 * species) + start, vector))
+                return carry
+
+            def four(m, carry):
+                for i in range(4):
+                    step(4 * m + i, carry)
+                return carry
+
+            lax.fori_loop(0, count // 4, four, 0)
+            for m in range(count // 4 * 4, count):
+                step(m, 0)
+
+        def store_even(m, value):
+            applied[pl.ds(pl.multiple_of(m * 8, 8), 8), :] = value
+
+        def store_odd(m, value):
+            at = pl.ds(pl.multiple_of(m * 8, 8), 8)
+            applied[at, :] = jnp.where(low_half, applied[at, :], value)
+
+        sweep(half + 1, 0, even[0:rows, :], store_even)
+        sweep(half, 4 * species - 4, odd[0:rows, :], store_odd)
+        tail_at = pl.ds(8 * half, 8)
+        applied[tail_at, :] = jnp.where(low_half, applied[tail_at, :], 0.0)
         return [
             padded(applied[pl.ds(2 * ct + x, ROWS, stride=4), :])
             for x in range(2)
@@ -367,9 +408,10 @@
     def reduce_stage(tile, turn, stage_id):
         at = turn % 2
         first, size, peer = ((0, boxes, box_peer), (boxes - 1, groups, grp_peer))[stage_id]
-        red_send[at, stage_id] = tile
+        high = tile.shape[0]
+        red_send[at, stage_id, 0:high] = tile
         copies = [
-            remote(red_send.at[at, stage_id], red_recv.at[at, first + k - 1],
+            remote(red_send.at[at, stage_id, 0:high], red_recv.at[at, first + k - 1, 0:high],
                    red_ssem.at[at, first + k - 1], red_rsem.at[at, first + k - 1], peer(k))
             for k in range(1, size)
         ]
@@ -381,7 +423,7 @@
             for copy in copies:
                 copy.wait_recv()
             for k in range(1, size):
-                total = total + red_recv[at, first + k - 1]
+                total = total + red_recv[at, first + k - 1, 0:high]
             for copy in copies:
                 copy.wait_send()
             return total
@@ -389,8 +431,9 @@
         return finish
 
     def reduce_rows(rows, turn):
-        row_id = iota((8, LANES), 0)
-        tile = jnp.zeros((8, LANES), F32)
+        high = -(-len(rows) // 8) * 8
+        row_id = iota((high, LANES), 0)
+        tile = jnp.zeros((high, LANES), F32)
         for i, row in enumerate(rows):
             tile = jnp.where(row_id == i, row, tile)
         return reduce_stage(tile, turn, 0)
@@ -446,11 +489,11 @@
 
         return flat, finish
 
-    for copy in ghost_copies:
-        copy.wait_send()
+    for_ghosts(lambda copy: copy.wait_send())
 
     direct[0], finish = send_halo(basis[0], 0)
     images[0] = finish()
+    gram = {}
     squares = []
     lengths = []
     columns = []
@@ -459,17 +502,32 @@
         image = images[j]
         known = [basis[i] for i in range(j + 1)]
         rows = [row_of(known[j], known[j])] + [row_of(v, image) for v in known]
+        rows += [row_of(v, known[j]) for v in known[:j]]
+        if not more:
+            rows.append(row_of(image, image))
         box_sums = reduce_rows(rows, j)
         if more:
             ahead, finish = send_halo(image, j + 1)
         all_sums = reduce_stage(box_sums(), j, 1)
         if more:
             ahead_image = finish()
+        else:
+            cell = iota((256, LANES), 0)
+            slot = iota((256, LANES), 1) & 63
+            to_slot = ((((cell >> 7) << 3) + ((cell & 127) >> 4)) >> 1) << 3
+            to_slot = ones_where(to_slot + ((cell & 15) >> 1) == slot)
+            means = []
+            for i in range(ITERS):
+                folded = direct[i, :, 0:256] + direct[i, :, 256:512]
+                mean = exact_dot(folded, to_slot, 3) * 0.125
+                means.append(jnp.where(left, mean[0:32], mean[32:64]))
         sums = sums_of(all_sums())
-        sums = [sums[i : i + 1] for i in range(j + 2)]
+        sums = [sums[i : i + 1] for i in range(len(rows))]
         squares.append(sums[0])
         lengths.append(jnp.sqrt(sums[0]))
         columns.append([sums[1 + i] / (lengths[i] * lengths[j]) for i in range(j + 1)])
+        for i in range(j):
+            gram[i, j] = sums[j + 2 + i]
         parts = [sums[1 + i] / (squares[i] * lengths[j]) for i in range(j + 1)]
         scale = 1.0 / lengths[j]
 
@@ -479,73 +537,57 @@
                 field = field - parts[i] * past[i]
             return field
 
-        basis[j + 1] = corrected(image, known)
         if more:
+            basis[j + 1] = corrected(image, known)
             direct[j + 1] = corrected(ahead, [direct[i] for i in range(j + 1)])
             images[j + 1] = corrected(ahead_image, [images[i] for i in range(j + 1)])
 
-    last = basis[ITERS]
-    box_sums = reduce_rows([row_of(last, last)], ITERS)
-    for j in range(ITERS - 1):
-        columns[j].append(lengths[j + 1])
-    upper, target, ending = rotated(columns, lengths[0])
-    none = jnp.zeros_like(lengths[0])
-    fixed = back_substitute(upper, target, none)
-    slope = back_substitute(upper, [none] * ITERS, none + 1.0)
-    means = []
-    cell = iota((256, LANES), 0)
-    slot = iota((256, LANES), 1) & 63
-    to_slot = (((((cell >> 7) << 3) + ((cell & 127) >> 4)) >> 1) << 3) + ((cell & 15) >> 1)
-    for solved in (fixed, slope):
-        total = sum((solved[j] / lengths[j]) * direct[j] for j in range(ITERS))
-        means.append(total[:, 0:256] + total[:, 256:512])
-    mean = exact_dot(jnp.concatenate(means, axis=0), ones_where(to_slot == slot), 3) * 0.125
-    left = iota((ROWS, LANES), 1) < 64
-    mean_send[...] = jnp.where(left, mean[0:ROWS], mean[SP : SP + ROWS])
-    all_sums = reduce_stage(box_sums(), ITERS, 1)
+    ratios = [sums[1 + i] / squares[i] for i in range(ITERS)]
+    square = sums[-1]
+    for i in range(ITERS):
+        square = square - ratios[i] * sums[1 + i]
+    for (i, k), entry in gram.items():
+        square = square + 2.0 * ratios[i] * ratios[k] * entry
+    length = jnp.sqrt(jnp.maximum(square, 0.0)) / lengths[ITERS - 1]
+    for j in range(ITERS):
+        columns[j].append((lengths + [length])[j + 1])
+    weights = least_squares(columns, lengths[0])
+    scales = [weights[j] / lengths[j] for j in range(ITERS)]
+    mean_send[...] = sum(scales[j] * means[j] for j in range(ITERS))
     mean_copies = [
         remote(mean_send, mean_recv.at[k - 1], mean_ssem.at[k - 1], mean_rsem.at[k - 1], grp_peer(k))
         for k in range(1, groups)
     ]
     for copy in mean_copies:
         copy.start()
-    length = jnp.sqrt(sums_of(all_sums())[0:1])
-    radius = jnp.sqrt(ending * ending + length * length)
-    final = (ending / radius) * target[ITERS - 1] / radius
-    weights = back_substitute(upper, target, final)
-    total = sum((weights[j] / lengths[j]) * direct[j] for j in range(ITERS))
+    total = sum(scales[j] * direct[j] for j in range(ITERS))
     for x in range(2):
         for ct in range(2):
             k = 2 * x + ct
-            flow[pl.ds(2 * ct + x, species, stride=4), :] = total[
+            correction_out[pl.ds(ct, species, stride=2), x, :] = total[
                 0:species, k * LANES : (k + 1) * LANES
             ]
-    flow_copy = pltpu.make_async_copy(
-        flow, correction_out.reshape(4 * species, LANES), load_sem.at[0]
-    )
-    flow_copy.start()
+    stage[...] = jnp.zeros_like(stage)
+    stage[0:species, 0:256] = coarse_raw[...]
+    blocks = [stage[:, c * LANES : (c + 1) * LANES] for c in range(2)]
     for copy in mean_copies:
         copy.wait_recv()
-    stage[...] = jnp.zeros_like(stage)
-    stage[0:species, 0:256] = coarse_raw[...]
-    blocks = [stage[0:ROWS, c * LANES : (c + 1) * LANES] for c in range(2)]
+    left_half = iota((SP, LANES), 1) < 64
     for k in range(groups):
         message = mean_send[...] if k == 0 else mean_recv[k - 1]
         turned = pltpu.roll(message, 64, 1)
-        message = jnp.where(left, message + final * turned, turned + final * message)
+        message = jnp.concatenate(
+            [jnp.where(left, message, turned), jnp.where(left, turned, message)], axis=0
+        )
         for c in range(2):
             entry = average_list[0, lax.rem(g + groups - k, groups)] - (4 * g + 2 * c)
             blocks[c] = jnp.where(
-                (left & (entry == 0)) | (~left & (entry == 1)), message, blocks[c]
+                (left_half & (entry == 0)) | (~left_half & (entry == 1)), message, blocks[c]
             )
     for c in range(2):
-        patch_new[:, c * LANES : (c + 1) * LANES] = blocks[c][0:species]
-    patch_copy = pltpu.make_async_copy(patch_new, coarse_out.at[:, 0, :], load_sem.at[1])
-    patch_copy.start()
+        coarse_out[:, 0, c * LANES : (c + 1) * LANES] = blocks[c][0:species]
     for copy in mean_copies:
         copy.wait_send()
-    flow_copy.wait()
-    patch_copy.wait()
 
 
 def on_device(
@@ -575,7 +617,7 @@
             jax.ShapeDtypeStruct((species, 1, 256), F32),
         ),
         in_specs=[smem, smem] + [hbm] * 8,
-        out_specs=(hbm, hbm),
+        out_specs=(pl.BlockSpec(memory_space=pltpu.VMEM),) * 2,
         scratch_shapes=[
             pltpu.VMEM((count, LANES), BF16),
             pltpu.VMEM((count + 4, LANES), F32),
@@ -599,18 +641,16 @@
             pltpu.VMEM((species, reactions), F32),
             pltpu.VMEM((4 * reactions, LANES), F32),
             pltpu.VMEM((species, 256), F32),
-            pltpu.VMEM((4 * species, LANES), F32),
-            pltpu.VMEM((species, 256), F32),
             pltpu.VMEM((2, 4, SP, LANES), F32),
-            pltpu.VMEM((groups - 1, ROWS, LANES), F32),
-            pltpu.VMEM((groups - 1, ROWS, LANES), F32),
+            pltpu.VMEM((groups - 1, 48, LANES), F32),
+            pltpu.VMEM((groups - 1, 48, LANES), F32),
             pltpu.VMEM((2, groups - 1, 16, LANES), F32),
             pltpu.VMEM((2, groups - 1, 16, LANES), F32),
             pltpu.VMEM((2, 2, 2, ROWS, LANES), F32),
-            pltpu.VMEM((2, 2, 8, LANES), F32),
-            pltpu.VMEM((2, reds, 8, LANES), F32),
-            pltpu.VMEM((ROWS, LANES), F32),
-            pltpu.VMEM((groups - 1, ROWS, LANES), F32),
+            pltpu.VMEM((2, 2, 16, LANES), F32),
+            pltpu.VMEM((2, reds, 16, LANES), F32),
+            pltpu.VMEM((32, LANES), F32),
+            pltpu.VMEM((groups - 1, 32, LANES), F32),
             dma((8,)),
             dma((groups - 1,)),
             dma((groups - 1,)),

time: 61.4 us -> 54.6 us (0.89)
  Pallas kernels: 57.6 us -> 50.7 us
    pallas_call x1, Pallas kernels: 57.6 us -> 50.7 us  [on_device(): pl.pallas_call(functools.partial(kernel, groups, boxes, species, reaction...]
where the time goes in v3:
time: 54.6 us; the launch traced here: 54.4 us
  Pallas kernels  50.7 us (93%)
  local copies, waits for them, and re-layouts  2.98 us (5%)
  between operations  0.64 us (1%)
    pallas_call x1, Pallas kernels, on_device(): pl.pallas_call(functools.partial(kernel, groups, boxes, species, reaction...  50.7 us
    unnamed x2, local copies, waits for them, and re-layouts  2.98 us

profile of v3, /device:TPU:0, one launch (start us, length us, event | category | flops | bytes accessed | tf_op | source)
XLA Modules:
  0.0 54.4 jit_solution(6257903768514057631)
XLA Ops:
  0.6 50.7 %gmres.1 = (f32[106,2,128]{2,1,0:T(2,128)}, f32[53,1,256]{2,1,0:T(1,128)}) custom-call(s32[4,8]{1,0:T(4,128)} %bitcast.29, s32[1,8]{1,0:T(1,128)} %bitcast.30, s32[8,1,160]{2,1,0:T(1,128)} %ghost_list.1, f32[106,2,128]{2,1,0:T(2,128)} %bitcast.26, f32[1,53]{1,0:T(1,128)} %bitcast.31, f32[53,325]{1,0:T(8,128)} %stoich.1, f32[53,325]{1,0:T(8,128)} %bitcast.28, ...), custom_call_target="tpu_custom_call" | custom-call | tf_op jit(solution)/shard_map/gmres/pallas_call | solution.py:613
  51.4 1.5 %copy.18 = f32[53,1,2,256]{3,2,1,0:T(2,128)} copy(f32[53,1,2,256]{3,2,1,0:T(2,128)} %bitcast.27) | data formatting | bytes 217088
  52.9 1.4 %copy.19 = f32[53,1,256]{2,1,0:T(1,128)} copy(f32[53,1,256]{2,1,0:T(1,128)} %get-tuple-element.9) | data formatting | bytes 108544

commit v4 on v3

--- a/solution.py
+++ b/solution.py
@@ -129,6 +129,9 @@
             device_id=device, device_id_type=MESH,
         )
 
+    def wait_bytes(ref, sem):
+        pltpu.make_async_copy(ref, ref, sem).wait()
+
     loads = [
         pltpu.make_async_copy(src, dst, load_sem.at[i])
         for i, (src, dst) in enumerate((
@@ -146,6 +149,23 @@
         load.start()
 
     stage[...] = jnp.zeros_like(stage)
+    even[...] = jnp.zeros_like(even)
+    odd[...] = jnp.zeros_like(odd)
+    applied[...] = jnp.zeros_like(applied)
+    rate[...] = jnp.zeros_like(rate)
+    x, y, z = cell_of(iota((512, LANES), 0))
+    slot = iota((512, LANES), 1)
+    pick[...] = ones_where(((slot >> 4 & 1) == x) & on_face(slot >> 5, slot & 15, y, z))
+    x, y, z = cell_of(iota((LANES, 512), 1))
+    slot = iota((LANES, 512), 0)
+    spread[...] = ones_where(((slot >> 4 & 1) == x) & on_face(slot >> 5, slot & 15, y, z))
+    end = jnp.where(b == 0, 0, 1)
+    behind_x = (slot < 64) & (x == end) & (((y >> 1) << 3) + (z >> 1) == slot)
+    past = slot - 64
+    face = past >> 3
+    t = jnp.where(face < 2, z, y)
+    behind_side = (slot >= 64) & (slot < 96) & ((t >> 1) == (past & 7)) & on_face(face, t, y, z)
+    coarse_spread = ones_where(behind_x | behind_side)
     loads[0].wait()
     loads[1].wait()
     stage[0:species, 0:256] = coarse_raw[...]
@@ -182,33 +202,27 @@
 
     for k in range(1, groups):
         ghost_send[k - 1] = chosen(k)
-    own_ghosts = chosen(0)
     pl.semaphore_wait(barrier, groups + boxes - 2)
 
     def ghost_copies(rows):
         return [
             remote(ghost_send.at[k - 1, 0:rows], ghost_recv.at[k - 1, 0:rows],
-                   ghost_ssem.at[k - 1], ghost_rsem.at[k - 1], grp_peer(k))
+                   ghost_ssem, ghost_rsem, grp_peer(k))
             for k in range(1, groups)
         ]
 
-    def for_ghosts(act):
-        @pl.when(at_end)
-        def _():
-            for copy in ghost_copies(48):
-                act(copy)
-
-        @pl.when(jnp.logical_not(at_end))
-        def _():
-            for copy in ghost_copies(16):
-                act(copy)
-
-    for_ghosts(lambda copy: copy.start())
-
-    even[...] = jnp.zeros_like(even)
-    odd[...] = jnp.zeros_like(odd)
-    applied[...] = jnp.zeros_like(applied)
-    rate[...] = jnp.zeros_like(rate)
+    def start_ghosts(rows):
+        for copy in ghost_copies(rows):
+            copy.start()
+
+    def wait_ghosts(ref, sem):
+        pl.when(at_end)(lambda: wait_bytes(ref.at[:, 0:48], sem))
+        pl.when(jnp.logical_not(at_end))(lambda: wait_bytes(ref.at[:, 0:16], sem))
+
+    pl.when(at_end)(lambda: start_ghosts(48))
+    pl.when(jnp.logical_not(at_end))(lambda: start_ghosts(16))
+    own_ghosts = chosen(0)
+
     for load in loads[3:]:
         load.wait()
     for x in range(2):
@@ -229,20 +243,6 @@
     stoich_high, stoich_low = split(whole, 2)
     stoich_cat[0:SP, :] = stoich_high
     stoich_cat[SP : 2 * SP, :] = stoich_low
-    x, y, z = cell_of(iota((512, LANES), 0))
-    slot = iota((512, LANES), 1)
-    pick[...] = ones_where(((slot >> 4 & 1) == x) & on_face(slot >> 5, slot & 15, y, z))
-    x, y, z = cell_of(iota((LANES, 512), 1))
-    slot = iota((LANES, 512), 0)
-    spread[...] = ones_where(((slot >> 4 & 1) == x) & on_face(slot >> 5, slot & 15, y, z))
-    end = jnp.where(b == 0, 0, 1)
-    behind_x = (slot < 64) & (x == end) & (((y >> 1) << 3) + (z >> 1) == slot)
-    past = slot - 64
-    face = past >> 3
-    t = jnp.where(face < 2, z, y)
-    behind_side = (slot >= 64) & (slot < 96) & ((t >> 1) == (past & 7)) & on_face(face, t, y, z)
-    coarse_spread = ones_where(behind_x | behind_side)
-
     loads[2].wait()
     count = species * species * 4
     chunk = 432
@@ -270,7 +270,7 @@
             stage[0:species, k * LANES : (k + 1) * LANES] = source_raw[
                 pl.ds(2 * ct + x, species, stride=4), :
             ]
-    for_ghosts(lambda copy: copy.wait_recv())
+    wait_ghosts(ghost_recv, ghost_rsem)
     side_part = own_ghosts[0:16]
     x_part = jnp.where(at_end, own_ghosts[16:48], 0.0)
     for k in range(1, groups):
@@ -412,7 +412,7 @@
         red_send[at, stage_id, 0:high] = tile
         copies = [
             remote(red_send.at[at, stage_id, 0:high], red_recv.at[at, first + k - 1, 0:high],
-                   red_ssem.at[at, first + k - 1], red_rsem.at[at, first + k - 1], peer(k))
+                   red_ssem.at[at, stage_id], red_rsem.at[at, stage_id], peer(k))
             for k in range(1, size)
         ]
         for copy in copies:
@@ -420,12 +420,11 @@
 
         def finish():
             total = tile
-            for copy in copies:
-                copy.wait_recv()
+            arrived = red_recv.at[at, first : first + size - 1, 0:high]
+            wait_bytes(arrived, red_rsem.at[at, stage_id])
             for k in range(1, size):
                 total = total + red_recv[at, first + k - 1, 0:high]
-            for copy in copies:
-                copy.wait_send()
+            wait_bytes(arrived, red_ssem.at[at, stage_id])
             return total
 
         return finish
@@ -455,8 +454,8 @@
         flat = jnp.concatenate(d, axis=1)
         side_messages(flat, at)
         plane_copies = [
-            remote(plane_send.at[at, k - 1], plane_recv.at[at, k - 1], plane_ssem.at[at, k - 1],
-                   plane_rsem.at[at, k - 1], grp_peer(k))
+            remote(plane_send.at[at, k - 1], plane_recv.at[at, k - 1], plane_ssem.at[at],
+                   plane_rsem.at[at], grp_peer(k))
             for k in range(1, groups)
         ]
         for copy in plane_copies:
@@ -478,18 +477,16 @@
             outer += [
                 padded(jnp.where(b < boxes - 1, x_recv[at, 1, ct], zero)) for ct in range(2)
             ]
-            for copy in plane_copies:
-                copy.wait_recv()
+            wait_bytes(plane_recv.at[at], plane_rsem.at[at])
             image = image - diffuse * (jnp.concatenate(outer, axis=1) + side_ghosts(at))
             pl.when(b < boxes - 1)(up.wait_send)
             pl.when(b > 0)(down.wait_send)
-            for copy in plane_copies:
-                copy.wait_send()
+            wait_bytes(plane_send.at[at], plane_ssem.at[at])
             return image
 
         return flat, finish
 
-    for_ghosts(lambda copy: copy.wait_send())
+    wait_ghosts(ghost_send, ghost_ssem)
 
     direct[0], finish = send_halo(basis[0], 0)
     images[0] = finish()
@@ -555,7 +552,7 @@
     scales = [weights[j] / lengths[j] for j in range(ITERS)]
     mean_send[...] = sum(scales[j] * means[j] for j in range(ITERS))
     mean_copies = [
-        remote(mean_send, mean_recv.at[k - 1], mean_ssem.at[k - 1], mean_rsem.at[k - 1], grp_peer(k))
+        remote(mean_send, mean_recv.at[k - 1], mean_ssem, mean_rsem, grp_peer(k))
         for k in range(1, groups)
     ]
     for copy in mean_copies:
@@ -570,8 +567,7 @@
     stage[...] = jnp.zeros_like(stage)
     stage[0:species, 0:256] = coarse_raw[...]
     blocks = [stage[:, c * LANES : (c + 1) * LANES] for c in range(2)]
-    for copy in mean_copies:
-        copy.wait_recv()
+    wait_bytes(mean_recv, mean_rsem)
     left_half = iota((SP, LANES), 1) < 64
     for k in range(groups):
         message = mean_send[...] if k == 0 else mean_recv[k - 1]
@@ -586,8 +582,18 @@
             )
     for c in range(2):
         coarse_out[:, 0, c * LANES : (c + 1) * LANES] = blocks[c][0:species]
-    for copy in mean_copies:
-        copy.wait_send()
+    wait_bytes(mean_recv, mean_ssem)
+
+
+def hand_over(correction, updated, correction_out, updated_out, sem):
+    copies = [
+        pltpu.make_async_copy(correction, correction_out, sem.at[0]),
+        pltpu.make_async_copy(updated, updated_out, sem.at[1]),
+    ]
+    for copy in copies:
+        copy.start()
+    for copy in copies:
+        copy.wait()
 
 
 def on_device(
@@ -652,16 +658,16 @@
             pltpu.VMEM((32, LANES), F32),
             pltpu.VMEM((groups - 1, 32, LANES), F32),
             dma((8,)),
-            dma((groups - 1,)),
-            dma((groups - 1,)),
-            dma((2, groups - 1)),
-            dma((2, groups - 1)),
+            dma,
+            dma,
+            dma((2,)),
+            dma((2,)),
             dma((2, 2)),
             dma((2, 2)),
-            dma((2, reds)),
-            dma((2, reds)),
-            dma((groups - 1,)),
-            dma((groups - 1,)),
+            dma((2, 2)),
+            dma((2, 2)),
+            dma,
+            dma,
         ],
         compiler_params=pltpu.CompilerParams(
             collective_id=0, has_side_effects=True, vmem_limit_bytes=63 * 1024 * 1024
@@ -679,6 +685,18 @@
         coarse_field,
         rows_of(precond),
     )
+    correction, updated = pl.pallas_call(
+        hand_over,
+        out_shape=(
+            jax.ShapeDtypeStruct((2 * species, 2, LANES), F32),
+            jax.ShapeDtypeStruct((species, 1, 256), F32),
+        ),
+        in_specs=[hbm] * 2,
+        out_specs=(hbm,) * 2,
+        scratch_shapes=[dma((2,))],
+        compiler_params=pltpu.CompilerParams(vmem_limit_bytes=63 * 1024 * 1024),
+        name="hand_over",
+    )(correction, updated)
     correction = correction.reshape(species, 2, 2, LANES).transpose(0, 2, 1, 3)
     return (correction.reshape(species, 1, 2, 256), updated)
 

time: 54.6 us -> 56.8 us (1.040)
  Pallas kernels: 50.7 us -> 56 us
  local copies, waits for them, and re-layouts: 2.98 us -> 0 us
    pallas_call x0 -> x1, Pallas kernels: none -> 6.05 us  [on_device(): pl.pallas_call(hand_over, out_shape=(jax.ShapeDtypeStruct((2 * species, 2...]
    unnamed x2 -> x0, local copies, waits for them, and re-layouts: 2.98 us -> none
    pallas_call x1, Pallas kernels: 50.7 us -> 50 us  [on_device(): pl.pallas_call(functools.partial(kernel, groups, boxes, species, reaction...]
where the time goes in v4:
time: 56.8 us; the launch traced here: 56.7 us
  Pallas kernels  56 us (99%)
  between operations  0.64 us (1%)
    pallas_call x1, Pallas kernels, on_device(): pl.pallas_call(functools.partial(kernel, groups, boxes, species, reaction...  50 us
    pallas_call x1, Pallas kernels, on_device(): pl.pallas_call(hand_over, out_shape=(jax.ShapeDtypeStruct((2 * species, 2...  6.05 us

profile of v4, /device:TPU:0, one launch (start us, length us, event | category | flops | bytes accessed | tf_op | source)
XLA Modules:
  0.0 56.7 jit_solution(3003836520833210840)
XLA Ops:
  0.6 50.0 %gmres.1 = (f32[106,2,128]{2,1,0:T(2,128)}, f32[53,1,256]{2,1,0:T(1,128)}) custom-call(s32[4,8]{1,0:T(4,128)} %bitcast.28, s32[1,8]{1,0:T(1,128)} %bitcast.29, s32[8,1,160]{2,1,0:T(1,128)} %ghost_list.1, f32[106,2,128]{2,1,0:T(2,128)} %bitcast.26, f32[1,53]{1,0:T(1,128)} %bitcast.30, f32[53,325]{1,0:T(8,128)} %stoich.1, f32[53,325]{1,0:T(8,128)} %bitcast.27, ...), custom_call_target="tpu_custom_call" | custom-call | tf_op jit(solution)/shard_map/gmres/pallas_call | solution.py:619
  50.6 6.1 %hand_over.1 = (f32[106,2,128]{2,1,0:T(2,128)}, f32[53,1,256]{2,1,0:T(1,128)}) custom-call(f32[106,2,128]{2,1,0:T(2,128)} %get-tuple-element.6.correction, f32[53,1,256]{2,1,0:T(1,128)} %get-tuple-element.7.updated), custom_call_target="tpu_custom_call" | custom-call | tf_op jit(solution)/shard_map/hand_over/pallas_call | solution.py:688

commit v5 on v4

--- a/solution.py
+++ b/solution.py
@@ -110,6 +110,7 @@
 ):
     g = lax.axis_index("grp")
     b = lax.axis_index("box")
+    used = -(-reactions // 16) * 16
     barrier = pltpu.get_barrier_semaphore()
 
     def grp_peer(k):
@@ -236,7 +237,7 @@
     whole = tall[...].T
     high = whole.astype(BF16).astype(F32)
     low = whole - high
-    order_parts = jnp.concatenate([high + pltpu.roll(low, 64, 1), high], axis=1).astype(BF16)
+    order_parts = jnp.concatenate([high + pltpu.roll(low, 64, 1), high], axis=1)[0:used].astype(BF16)
     stage[...] = jnp.zeros_like(stage)
     stage[0:species, 0:reactions] = stoich_raw[...]
     whole = stage[:, 0:RP]
@@ -464,10 +465,10 @@
         def finish():
             d_high, d_low = split(flat, 2)
             d_cat = jnp.concatenate([d_high, d_high, d_low, jnp.zeros_like(d_low)], axis=0)
-            progress = rate[...] * dot(order_parts, d_cat)
+            progress = rate[0:used, :] * dot(order_parts, d_cat)
             q_high, q_low = split(progress, 2)
-            both = dot(stoich_cat[...], q_high)
-            chemistry = both[0:SP] + both[SP:] + dot(stoich_cat[0:SP, :], q_low)
+            both = dot(stoich_cat[:, 0:used], q_high)
+            chemistry = both[0:SP] + both[SP:] + dot(stoich_cat[0:SP, 0:used], q_low)
             inner = jnp.concatenate(inner_sum(d), axis=1)
             image = flat + diffuse * (6.0 * flat - inner) - chemistry
             pl.when(b > 0)(up.wait_recv)
@@ -585,14 +586,21 @@
     wait_bytes(mean_recv, mean_ssem)
 
 
-def hand_over(correction, updated, correction_out, updated_out, sem):
-    copies = [
-        pltpu.make_async_copy(correction, correction_out, sem.at[0]),
-        pltpu.make_async_copy(updated, updated_out, sem.at[1]),
+def hand_over(correction, updated, correction_out, updated_out, held, held_patch, sem):
+    inward = [
+        pltpu.make_async_copy(correction, held, sem.at[0]),
+        pltpu.make_async_copy(updated, held_patch, sem.at[1]),
     ]
-    for copy in copies:
+    outward = [
+        pltpu.make_async_copy(held, correction_out, sem.at[2]),
+        pltpu.make_async_copy(held_patch, updated_out, sem.at[3]),
+    ]
+    for copy in inward:
         copy.start()
-    for copy in copies:
+    for copy, following in zip(inward, outward):
+        copy.wait()
+        following.start()
+    for copy in outward:
         copy.wait()
 
 
@@ -693,7 +701,11 @@
         ),
         in_specs=[hbm] * 2,
         out_specs=(hbm,) * 2,
-        scratch_shapes=[dma((2,))],
+        scratch_shapes=[
+            pltpu.VMEM((2 * species, 2, LANES), F32),
+            pltpu.VMEM((species, 1, 256), F32),
+            dma((4,)),
+        ],
         compiler_params=pltpu.CompilerParams(vmem_limit_bytes=63 * 1024 * 1024),
         name="hand_over",
     )(correction, updated)

time: 56.8 us -> 52.4 us (0.923)
  Pallas kernels: 56 us -> 51.6 us
    pallas_call x1, Pallas kernels: 6.05 us -> 1.59 us  [on_device(): pl.pallas_call(hand_over, out_shape=(jax.ShapeDtypeStruct((2 * species, 2...]
where the time goes in v5:
time: 52.4 us; the launch traced here: 52.2 us
  Pallas kernels  51.6 us (98%)
  between operations  0.64 us (1%)
    pallas_call x1, Pallas kernels, on_device(): pl.pallas_call(functools.partial(kernel, groups, boxes, species, reaction...  50 us
    pallas_call x1, Pallas kernels, on_device(): pl.pallas_call(hand_over, out_shape=(jax.ShapeDtypeStruct((2 * species, 2...  1.59 us

profile of v5, /device:TPU:0, one launch (start us, length us, event | category | flops | bytes accessed | tf_op | source)
XLA Modules:
  0.0 52.2 jit_solution(11072777001784117846)
XLA Ops:
  0.6 50.0 %gmres.1 = (f32[106,2,128]{2,1,0:T(2,128)}, f32[53,1,256]{2,1,0:T(1,128)}) custom-call(s32[4,8]{1,0:T(4,128)} %bitcast.28, s32[1,8]{1,0:T(1,128)} %bitcast.29, s32[8,1,160]{2,1,0:T(1,128)} %ghost_list.1, f32[106,2,128]{2,1,0:T(2,128)} %bitcast.26, f32[1,53]{1,0:T(1,128)} %bitcast.30, f32[53,325]{1,0:T(8,128)} %stoich.1, f32[53,325]{1,0:T(8,128)} %bitcast.27, ...), custom_call_target="tpu_custom_call" | custom-call | tf_op jit(solution)/shard_map/gmres/pallas_call | solution.py:627
  50.6 1.6 %hand_over.1 = (f32[106,2,128]{2,1,0:T(2,128)}, f32[53,1,256]{2,1,0:T(1,128)}) custom-call(f32[106,2,128]{2,1,0:T(2,128)} %get-tuple-element.6.correction, f32[53,1,256]{2,1,0:T(1,128)} %get-tuple-element.7.updated), custom_call_target="tpu_custom_call" | custom-call | tf_op jit(solution)/shard_map/hand_over/pallas_call | solution.py:696
